TPU v7x, 32 devices: a whole 2x2x4 slice. The times are simulated.
32 devices in a mesh: seq: 16 (over z, y, core), head: 2 (over x).
Axes of the slice: x: 2, y: 2, z: 4, core: 2. Of those that a mesh axis runs over, the one named last changes fastest.
Arguments:
- queries: bfloat16 [8192, 4096], P(('seq', 'head')), may hold values from -25 to 25
- key_rows: bfloat16 [8192, 4096], P(('seq', 'head')), may hold values from -6 to 6
- value_rows: bfloat16 [8192, 4096], P(('seq', 'head')), may hold values from -6 to 6
- out_grad: bfloat16 [8192, 4096], P(('seq', 'head')), may hold values from -6 to 6
- doc_ids: int32 [8192], replicated, may hold values from 0 to 3, never falling along the last dimension, each value on 1 to 4096 neighbouring positions
- picks: int32 [16, 32, 2], P('seq', 'head'), may hold values from 1 to 3, as said below
Outputs:
- attn_out: bfloat16 [8192, 4096], P(('seq', 'head'))
- query_grad: bfloat16 [8192, 4096], P(('seq', 'head'))
- key_grad: bfloat16 [8192, 4096], P(('seq', 'head'))
- value_grad: bfloat16 [8192, 4096], P(('seq', 'head'))
Inputs may be any that keep to these rules, and one draw needn't show every extreme that they name: `doc_ids`: never falling along the tokens; each document is at most 4096 tokens, one exactly that long. `picks`: for each block and head, 2 different offsets.
All inputs are finite; a program needn't handle non-finite values.
Results may differ from a plain program's by a relative error of at most 0.027.
Values may be sent and summed in bfloat16 or wider, within the bound.
A program may use at most 128 MiB of HBM per device.

v0:
```python
import jax
import jax.numpy as jnp
from jax import lax
from jax.sharding import PartitionSpec as P

HEAD_DIM = 128
BLOCK = 512
REACH = 3


NEGATIVE = -1e30


def shifted(shard, axis, by):
    length = lax.axis_size(axis)
    pairs = [(i, i + by) for i in range(length) if 0 <= i + by < length]
    return lax.ppermute(shard, axis, pairs)


def block_masks(picks_block, own_index, docs_query, docs_window):
    head_count = picks_block.shape[0]
    slot_count = docs_window.shape[0]
    block_rows = docs_query.shape[0]
    chosen = jnp.concatenate(
        [own_index - picks_block, jnp.full((head_count, 1), own_index, jnp.int32)], axis=1
    )
    onehot = chosen[:, :, None] == jnp.arange(slot_count, dtype=jnp.int32)[None, None, :]
    docs_chosen = docs_window[chosen]
    key_count = chosen.shape[1]
    causal = jnp.arange(block_rows)[None, :] <= jnp.arange(block_rows)[:, None]
    earlier = jnp.arange(key_count) < key_count - 1
    allowed = jnp.logical_or(earlier[None, :, None], causal[:, None, :])
    same_doc = docs_query[None, :, None, None] == docs_chosen[:, None, :, :]
    return (onehot, jnp.logical_and(same_doc, allowed[None]))


def choose_rows(onehot, window):
    picked = jnp.einsum(
        "hkw,wbhe->hkbe", onehot.astype(jnp.bfloat16), window, preferred_element_type=jnp.float32
    )
    return picked.astype(jnp.bfloat16)


def masked_scores(query_head, keys_head, mask_head, score_scale):
    scores = (
        jnp.einsum("be,kce->bkc", query_head, keys_head, preferred_element_type=jnp.float32)
        * score_scale
    )
    return jnp.where(mask_head, scores, NEGATIVE)


def forward_heads(query_block, keys_chosen, values_chosen, allowed_mask, score_scale):

    def forward_one_head(pieces):
        query_head, keys_head, values_head, mask_head = pieces
        scores = masked_scores(query_head, keys_head, mask_head, score_scale)
        row_max = jnp.max(scores, axis=(1, 2), keepdims=True)
        row_total = jnp.sum(jnp.exp(scores - row_max), axis=(1, 2), keepdims=True)
        log_total = row_max + jnp.log(row_total)
        probs_low = jnp.exp(scores - log_total).astype(jnp.bfloat16)
        result = jnp.einsum(
            "bkc,kce->be", probs_low, values_head, preferred_element_type=jnp.float32
        ).astype(jnp.bfloat16)
        return (result, log_total[:, 0, 0])

    results, logs = lax.map(
        forward_one_head,
        (jnp.swapaxes(query_block, 0, 1), keys_chosen, values_chosen, allowed_mask),
    )
    return (jnp.swapaxes(results, 0, 1), logs)


def backward_heads(
    query_block,
    grad_block,
    out_block,
    log_block,
    keys_chosen,
    values_chosen,
    allowed_mask,
    onehot,
    score_scale,
):

    def backward_one_head(pieces):
        query_head, grad_head, out_head, log_head, keys_head, values_head, mask_head, place_head = (
            pieces
        )
        scores = masked_scores(query_head, keys_head, mask_head, score_scale)
        probs_full = jnp.exp(scores - log_head[:, None, None])
        probs_low = probs_full.astype(jnp.bfloat16)
        delta = jnp.sum(grad_head.astype(jnp.float32) * out_head.astype(jnp.float32), axis=1)
        prob_grad = jnp.einsum(
            "be,kce->bkc", grad_head, values_head, preferred_element_type=jnp.float32
        )
        score_grad = (probs_full * (prob_grad - delta[:, None, None]) * score_scale).astype(
            jnp.bfloat16
        )
        query_part = jnp.einsum(
            "bkc,kce->be", score_grad, keys_head, preferred_element_type=jnp.float32
        )
        key_part = jnp.einsum(
            "bkc,be->kce", score_grad, query_head, preferred_element_type=jnp.float32
        )
        value_part = jnp.einsum(
            "bkc,be->kce", probs_low, grad_head, preferred_element_type=jnp.float32
        )
        placing = place_head.astype(jnp.float32)
        key_slots = jnp.einsum("kw,kce->wce", placing, key_part, precision=lax.Precision.HIGHEST)
        value_slots = jnp.einsum(
            "kw,kce->wce", placing, value_part, precision=lax.Precision.HIGHEST
        )
        return (query_part, key_slots, value_slots)

    query_parts, key_slots, value_slots = lax.map(
        backward_one_head,
        (
            jnp.swapaxes(query_block, 0, 1),
            jnp.swapaxes(grad_block, 0, 1),
            jnp.swapaxes(out_block, 0, 1),
            log_block,
            keys_chosen,
            values_chosen,
            allowed_mask,
            onehot,
        ),
    )
    return (
        jnp.swapaxes(query_parts, 0, 1),
        jnp.transpose(key_slots, (1, 2, 0, 3)),
        jnp.transpose(value_slots, (1, 2, 0, 3)),
    )


def per_device(queries, key_rows, value_rows, out_grad, doc_ids, picks):
    head_total = queries.shape[1] // HEAD_DIM
    head_count = head_total // lax.axis_size("head")
    feature_width = head_count * HEAD_DIM
    row_count = queries.shape[0] * lax.axis_size("head")
    block_count = row_count // BLOCK
    shifts = (REACH + block_count - 1) // block_count
    slot_count = (shifts + 1) * block_count
    score_scale = HEAD_DIM ** (-0.5)

    def shaped(array):
        return array.reshape(-1, BLOCK, head_count, HEAD_DIM)

    query_all, key_all, value_all, grad_all = (
        lax.all_to_all(queries, "head", split_axis=1, concat_axis=0, tiled=True),
        lax.all_to_all(key_rows, "head", split_axis=1, concat_axis=0, tiled=True),
        lax.all_to_all(value_rows, "head", split_axis=1, concat_axis=0, tiled=True),
        lax.all_to_all(out_grad, "head", split_axis=1, concat_axis=0, tiled=True),
    )
    earlier_keys_list = []
    earlier_values_list = []
    for offset in range(shifts, 0, -1):
        moved_keys, moved_values = shifted((key_all, value_all), "seq", offset)
        earlier_keys_list.append(moved_keys)
        earlier_values_list.append(moved_values)
    key_window = shaped(jnp.concatenate(earlier_keys_list + [key_all], axis=0))
    value_window = shaped(jnp.concatenate(earlier_values_list + [value_all], axis=0))
    seq_index = lax.axis_index("seq")
    docs_pad = jnp.concatenate([jnp.full((shifts * row_count,), -1, jnp.int32), doc_ids])
    docs_window = lax.dynamic_slice_in_dim(
        docs_pad, seq_index * row_count, slot_count * BLOCK, 0
    ).reshape(slot_count, BLOCK)
    query_blocks = shaped(query_all)
    grad_blocks = shaped(grad_all)
    local = 0
    own_index = shifts * block_count + local
    setups = [block_masks(picks[local], own_index, docs_window[own_index], docs_window)]
    local = 0
    onehot, allowed_mask = setups[local]
    out_block, log_block = forward_heads(
        query_blocks[local],
        choose_rows(onehot, key_window),
        choose_rows(onehot, value_window),
        allowed_mask,
        score_scale,
    )
    out_blocks = [out_block]
    log_blocks = [log_block]
    attn_heads = out_blocks[0].reshape(row_count, feature_width)
    attn_out = lax.all_to_all(attn_heads, "head", split_axis=0, concat_axis=1, tiled=True)
    local = 0
    onehot, allowed_mask = setups[local]
    query_part, key_slots, value_slots = backward_heads(
        query_blocks[local],
        grad_blocks[local],
        out_blocks[local],
        log_blocks[local],
        choose_rows(onehot, key_window),
        choose_rows(onehot, value_window),
        allowed_mask,
        onehot,
        score_scale,
    )
    query_parts = query_part.astype(jnp.bfloat16)
    query_heads = query_parts.reshape(row_count, feature_width)
    key_low = key_slots.astype(jnp.bfloat16).reshape(slot_count * BLOCK, feature_width)
    value_low = value_slots.astype(jnp.bfloat16).reshape(slot_count * BLOCK, feature_width)
    key_total = key_low[shifts * row_count :].astype(jnp.float32)
    value_total = value_low[shifts * row_count :].astype(jnp.float32)
    for offset in range(1, shifts + 1):
        row_start = (shifts - offset) * row_count
        back_key, back_value = shifted(
            (
                key_low[row_start : row_start + row_count],
                value_low[row_start : row_start + row_count],
            ),
            "seq",
            -offset,
        )
        key_total = key_total + back_key.astype(jnp.float32)
        value_total = value_total + back_value.astype(jnp.float32)
    query_grad, key_grad, value_grad = (
        lax.all_to_all(query_heads, "head", split_axis=0, concat_axis=1, tiled=True),
        lax.all_to_all(
            key_total.astype(jnp.bfloat16), "head", split_axis=0, concat_axis=1, tiled=True
        ),
        lax.all_to_all(
            value_total.astype(jnp.bfloat16), "head", split_axis=0, concat_axis=1, tiled=True
        ),
    )
    return (attn_out, query_grad, key_grad, value_grad)


def solution(mesh):
    placed = (
        P(("seq", "head"), None),
        P(("seq", "head"), None),
        P(("seq", "head"), None),
        P(("seq", "head"), None),
        P(),
        P("seq", "head", None),
    )
    return jax.shard_map(
        per_device,
        mesh=mesh,
        in_specs=placed,
        out_specs=(
            P(("seq", "head"), None),
            P(("seq", "head"), None),
            P(("seq", "head"), None),
            P(("seq", "head"), None),
        ),
        check_vma=False,
    )
```

profile of v0, /device:TPU:23, one launch (start us, length us, event | category | flops | bytes accessed | tf_op | source)
XLA Modules:
  0.0 941.8 jit_solution(8393205909248707284)
XLA Ops:
  11.9 19.0 %all-to-all-done = bf16[256,2,2048]{2,0,1:T(8,128)(2,1)S(1)} async-done(((bf16[256,2,2048]{2,0,1:T(8,128)(2,1)}), bf16[256,2,2048]{2,0,1:T(8,128)(2,1)S(1)}, u32[]{:S(2)}, u32[]{:S(2)}) %all-to-all-start) | async-done | bytes 2097184 | tf_op jit(solution)/shard_map/all_to_all | solution.py:149
  40.9 18.2 %all-to-all-done.2 = bf16[256,2,2048]{0,2,1:T(8,128)(2,1)} async-done(((bf16[256,2,2048]{0,2,1:T(8,128)(2,1)}), bf16[256,2,2048]{0,2,1:T(8,128)(2,1)}, u32[]{:S(2)}, u32[]{:S(2)}) %all-to-all-start.2) | async-done | bytes 2097184 | tf_op jit(solution)/shard_map/all_to_all | solution.py:151
  92.4 10.5 %compare_and_fusion = pred[16,512,3,512]{3,1,2,0:T(32,128)(4,1)} fusion(s32[16,3,512]{2,1,0:T(4,128)S(1)} %reshape.122, s32[512]{0:T(512)S(1)} %pad_dynamic-slice_fusion, pred[512,3,512]{2,0,1:T(8,128)(4,1)S(1)} %broadcast_or_fusion), kind=kLoop, calls=%fused_computation.57 | loop fusion | flops 25165824 | bytes 13469696 | tf_op jit(solution)/shard_map/and | solution.py:34
  107.0 6.7 collective-permute-start.2
  127.7 40.9 %collective-permute-done.4 = bf16[512,2048]{1,0:T(8,128)(2,1)} collective-permute-done((bf16[512,2048]{1,0:T(8,128)(2,1)}, bf16[512,2048]{1,0:T(8,128)(2,1)}, u32[]{:S(2)}, u32[]{:S(2)}) %collective-permute-start.4) | collective-permute-done | bytes 2097184 | tf_op jit(solution)/shard_map/ppermute | solution.py:17
  168.6 44.0 %collective-permute-done.3 = bf16[512,2048]{1,0:T(8,128)(2,1)} collective-permute-done((bf16[512,2048]{1,0:T(8,128)(2,1)}, bf16[512,2048]{1,0:T(8,128)(2,1)}, u32[]{:S(2)}, u32[]{:S(2)}) %collective-permute-start.3) | collective-permute-done | bytes 2097184 | tf_op jit(solution)/shard_map/ppermute | solution.py:17
  212.6 7.1 maximum_bitcast_fusion.1
  219.6 9.7 %copy.99 = bf16[256,8,16,128]{3,2,1,0:T(8,128)(2,1)} copy(bf16[256,8,16,128]{3,1,2,0:T(8,128)(2,1)} %maximum_bitcast_fusion.1) | data formatting | bytes 16777216
  229.4 10.5 %fusion.50 = bf16[16,3,512,128]{3,1,2,0:T(4,128)(2,1)S(1)} fusion(bf16[4,512,16,128]{3,2,1,0:T(8,128)(2,1)} %bitcast.200, s32[16,3]{1,0:T(8,128)S(1)} %concatenate.13.clone), kind=kOutput, calls=%fused_computation.67 | convolution fusion | flops 28311744 | bytes 14680256 | tf_op jit(solution)/shard_map/hkw,wbhe->hkbe/dot_general | solution.py:38
  244.2 13.3 %collective-permute-done.2 = bf16[512,2048]{1,0:T(8,128)(2,1)} collective-permute-done((bf16[512,2048]{1,0:T(8,128)(2,1)}, bf16[512,2048]{1,0:T(8,128)(2,1)}, u32[]{:S(2)}, u32[]{:S(2)}) %collective-permute-start.2) | collective-permute-done | bytes 2097184 | tf_op jit(solution)/shard_map/ppermute | solution.py:17
  257.5 25.0 %collective-permute-done.1 = bf16[512,2048]{1,0:T(8,128)(2,1)} collective-permute-done((bf16[512,2048]{1,0:T(8,128)(2,1)}, bf16[512,2048]{1,0:T(8,128)(2,1)}, u32[]{:S(2)}, u32[]{:S(2)}) %collective-permute-start.1) | collective-permute-done | bytes 2097184 | tf_op jit(solution)/shard_map/ppermute | solution.py:17
  282.6 22.4 %collective-permute-done = bf16[512,2048]{1,0:T(8,128)(2,1)S(1)} collective-permute-done((bf16[512,2048]{1,0:T(8,128)(2,1)S(1)}, bf16[512,2048]{1,0:T(8,128)(2,1)S(1)}, u32[]{:S(2)}, u32[]{:S(2)}) %collective-permute-start) | collective-permute-done | bytes 2097184 | tf_op jit(solution)/shard_map/ppermute | solution.py:17
  304.9 6.6 maximum_bitcast_fusion
  311.5 9.7 %copy.98 = bf16[256,8,16,128]{3,2,1,0:T(8,128)(2,1)} copy(bf16[256,8,16,128]{3,1,2,0:T(8,128)(2,1)} %maximum_bitcast_fusion) | data formatting | bytes 16777216
  321.3 10.6 %fusion.47 = bf16[16,3,512,128]{3,1,2,0:T(4,128)(2,1)S(1)} fusion(bf16[4,512,16,128]{3,2,1,0:T(8,128)(2,1)} %bitcast.199, s32[16,3]{1,0:T(8,128)S(1)} %concatenate.13.clone), kind=kOutput, calls=%fused_computation.66 | convolution fusion | flops 28311744 | bytes 14680256 | tf_op jit(solution)/shard_map/hkw,wbhe->hkbe/dot_general | solution.py:38
  336.3 107.6 %while.26 = (s32[]{:T(128)}, bf16[16,512,128]{2,1,0:T(8,128)(2,1)}, f32[16,512]{1,0:T(8,128)S(1)}, pred[16,512,3,512]{3,1,2,0:T(32,128)(4,1)}, bf16[16,512,128]{...) while((s32[]{:T(128)}, bf16[16,512,128]{2,1,0:T(8,128)(2,1)}, ...), condition=%wide.region_3.4_spmd, body=%wide.region_0.3_spmd.sunk | while | flops 408223232 | bytes 14438509 | solution.py:66
  444.0 246.6 %while.27 = (s32[]{:T(128)}, bf16[16,512,128]{2,1,0:T(8,128)(2,1)}, bf16[16,4,512,128]{2,3,0,1:T(8,128)(2,1)}, bf16[16,4,512,128]{2,3,0,1:T(8,128)(2,1)}, pred[1...) while((s32[]{:T(128)}, bf16[16,512,128]{2,1,0:T(8,128)(2,1)}, ...), condition=%wide.region_6.7_spmd, body=%wide.region_4.6_spmd.sunk | while | flops 1032060416 | bytes 25574048 | solution.py:115
  690.6 6.2 fusion.62
  722.8 18.2 %collective-permute-done.11 = bf16[512,2048]{0,1:T(8,128)(2,1)} collective-permute-done((bf16[512,2048]{0,1:T(8,128)(2,1)}, bf16[512,2048]{0,1:T(8,128)(2,1)}, u32[]{:S(2)}, u32[]{:S(2)}) %collective-permute-start.11) | collective-permute-done | bytes 2097184 | tf_op jit(solution)/shard_map/ppermute | solution.py:17
  741.0 7.7 collective-permute-start.6
  762.1 28.9 %collective-permute-done.10 = bf16[512,2048]{0,1:T(8,128)(2,1)} collective-permute-done((bf16[512,2048]{0,1:T(8,128)(2,1)}, bf16[512,2048]{0,1:T(8,128)(2,1)}, u32[]{:S(2)}, u32[]{:S(2)}) %collective-permute-start.10) | collective-permute-done | bytes 2097184 | tf_op jit(solution)/shard_map/ppermute | solution.py:17
  808.0 22.8 %collective-permute-done.8 = bf16[512,2048]{0,1:T(8,128)(2,1)} collective-permute-done((bf16[512,2048]{0,1:T(8,128)(2,1)}, bf16[512,2048]{0,1:T(8,128)(2,1)}, u32[]{:S(2)}, u32[]{:S(2)}) %collective-permute-start.8) | collective-permute-done | bytes 2097184 | tf_op jit(solution)/shard_map/ppermute | solution.py:17
  830.8 50.3 %collective-permute-done.7 = bf16[512,2048]{0,1:T(8,128)(2,1)} collective-permute-done((bf16[512,2048]{0,1:T(8,128)(2,1)}, bf16[512,2048]{0,1:T(8,128)(2,1)}, u32[]{:S(2)}, u32[]{:S(2)}) %collective-permute-start.7) | collective-permute-done | bytes 2097184 | tf_op jit(solution)/shard_map/ppermute | solution.py:17
  881.2 24.6 %collective-permute-done.6 = bf16[512,2048]{0,1:T(8,128)(2,1)} collective-permute-done((bf16[512,2048]{0,1:T(8,128)(2,1)}, bf16[512,2048]{0,1:T(8,128)(2,1)}, u32[]{:S(2)}, u32[]{:S(2)}) %collective-permute-start.6) | collective-permute-done | bytes 2097184 | tf_op jit(solution)/shard_map/ppermute | solution.py:17
  (394 shorter events, 525.9 us)
Async XLA Ops:
  3.8 27.1 %all-to-all-start = ((bf16[256,2,2048]{2,0,1:T(8,128)(2,1)}), bf16[256,2,2048]{2,0,1:T(8,128)(2,1)S(1)}, u32[]{:S(2)}, u32[]{:S(2)}) async-start(bf16[256,2,2048]{2,0,1:T(8,128)(2,1)} %bitcast.208), calls=%async_computation | async-start | bytes 4194304 | tf_op jit(solution)/shard_map/all_to_all | solution.py:149
  30.9 28.2 %all-to-all-start.2 = ((bf16[256,2,2048]{0,2,1:T(8,128)(2,1)}), bf16[256,2,2048]{0,2,1:T(8,128)(2,1)}, u32[]{:S(2)}, u32[]{:S(2)}) async-start(bf16[256,2,2048]{0,2,1:T(8,128)(2,1)} %bitcast.207), calls=%async_computation.2 | async-start | bytes 4194304 | tf_op jit(solution)/shard_map/all_to_all | solution.py:151
  40.9 24.2 %copy-start.6 = (s32[1,16,2]{1,2,0:T(2,128)S(1)}, s32[1,16,2]{1,2,0:T(2,128)}, u32[]{:S(2)}) copy-start(s32[1,16,2]{1,2,0:T(2,128)} %param.15) | copy-start | bytes 388
  40.9 24.4 %copy-start.5 = (s32[8192]{0:T(1024)S(1)}, s32[8192]{0:T(1024)}, u32[]{:S(2)}) copy-start(s32[8192]{0:T(1024)} %param.14) | copy-start | bytes 98308
  59.1 27.3 %all-to-all-start.1 = ((bf16[256,2,2048]{0,2,1:T(8,128)(2,1)}), bf16[256,2,2048]{0,2,1:T(8,128)(2,1)}, u32[]{:S(2)}, u32[]{:S(2)}) async-start(bf16[256,2,2048]{0,2,1:T(8,128)(2,1)} %bitcast.203), calls=%async_computation.1 | async-start | bytes 4194304 | tf_op jit(solution)/shard_map/all_to_all | solution.py:150
  73.7 49.7 %collective-permute-start.5 = (bf16[512,2048]{1,0:T(8,128)(2,1)}, bf16[512,2048]{1,0:T(8,128)(2,1)}, u32[]{:S(2)}, u32[]{:S(2)}) collective-permute-start(bf16[512,2048]{1,0:T(8,128)(2,1)} %bitcast.215), channel_id=1, source_target_pairs={{0,2},{2,4},{4,6},{6,8},{8,10},{10,12},{12,14},{14,16},{16,18},{18... | collective-permute-start | bytes 6291464 | tf_op jit(solution)/shard_map/ppermute | solution.py:17
  79.5 89.1 %collective-permute-start.4 = (bf16[512,2048]{1,0:T(8,128)(2,1)}, bf16[512,2048]{1,0:T(8,128)(2,1)}, u32[]{:S(2)}, u32[]{:S(2)}) collective-permute-start(bf16[512,2048]{1,0:T(8,128)(2,1)} %bitcast.216), channel_id=1, source_target_pairs={{0,4},{2,6},{4,8},{6,10},{8,12},{10,14},{12,16},{14,18},{16,20},{1... | collective-permute-start | bytes 6291464 | tf_op jit(solution)/shard_map/ppermute | solution.py:17
  82.7 129.9 %collective-permute-start.3 = (bf16[512,2048]{1,0:T(8,128)(2,1)}, bf16[512,2048]{1,0:T(8,128)(2,1)}, u32[]{:S(2)}, u32[]{:S(2)}) collective-permute-start(bf16[512,2048]{1,0:T(8,128)(2,1)} %bitcast.217), channel_id=1, source_target_pairs={{0,6},{2,8},{4,10},{6,12},{8,14},{10,16},{12,18},{14,20},{16,22},{... | collective-permute-start | bytes 6291464 | tf_op jit(solution)/shard_map/ppermute | solution.py:17
  86.4 32.9 %all-to-all-start.4 = ((bf16[256,2,2048]{2,0,1:T(8,128)(2,1)}), bf16[256,2,2048]{2,0,1:T(8,128)(2,1)}, u32[]{:S(2)}, u32[]{:S(2)}) async-start(bf16[256,2,2048]{2,0,1:T(8,128)(2,1)} %bitcast.204), calls=%async_computation.4 | async-start | bytes 4194304 | tf_op jit(solution)/shard_map/all_to_all | solution.py:152
  107.0 150.5 %collective-permute-start.2 = (bf16[512,2048]{1,0:T(8,128)(2,1)}, bf16[512,2048]{1,0:T(8,128)(2,1)}, u32[]{:S(2)}, u32[]{:S(2)}) collective-permute-start(bf16[512,2048]{1,0:T(8,128)(2,1)} %bitcast.219), channel_id=1, source_target_pairs={{0,2},{2,4},{4,6},{6,8},{8,10},{10,12},{12,14},{14,16},{16,18},{18... | collective-permute-start | bytes 6291464 | tf_op jit(solution)/shard_map/ppermute | solution.py:17
  113.7 168.9 %collective-permute-start.1 = (bf16[512,2048]{1,0:T(8,128)(2,1)}, bf16[512,2048]{1,0:T(8,128)(2,1)}, u32[]{:S(2)}, u32[]{:S(2)}) collective-permute-start(bf16[512,2048]{1,0:T(8,128)(2,1)} %bitcast.220), channel_id=1, source_target_pairs={{0,4},{2,6},{4,8},{6,10},{8,12},{10,14},{12,16},{14,18},{16,20},{1... | collective-permute-start | bytes 6291464 | tf_op jit(solution)/shard_map/ppermute | solution.py:17
  121.5 91.0 %copy-start.2 = (bf16[2,256,2048]{2,1,0:T(8,128)(2,1)S(1)}, bf16[2,256,2048]{2,1,0:T(8,128)(2,1)}, u32[]{:S(2)}) copy-start(bf16[2,256,2048]{2,1,0:T(8,128)(2,1)} %copy.57) | copy-start | bytes 6291460
  123.5 181.5 %collective-permute-start = (bf16[512,2048]{1,0:T(8,128)(2,1)S(1)}, bf16[512,2048]{1,0:T(8,128)(2,1)S(1)}, u32[]{:S(2)}, u32[]{:S(2)}) collective-permute-start(bf16[512,2048]{1,0:T(8,128)(2,1)S(1)} %bitcast.221), channel_id=1, source_target_pairs={{0,6},{2,8},{4,10},{6,12},{8,14},{10,16},{12,18},{14,20},{16,22},{... | collective-permute-start | bytes 6291464 | tf_op jit(solution)/shard_map/ppermute | solution.py:17
  696.8 44.2 %collective-permute-start.11 = (bf16[512,2048]{0,1:T(8,128)(2,1)}, bf16[512,2048]{0,1:T(8,128)(2,1)}, u32[]{:S(2)}, u32[]{:S(2)}) collective-permute-start(bf16[512,2048]{0,1:T(8,128)(2,1)} %bitcast.56), channel_id=1, source_target_pairs={{6,0},{8,2},{10,4},{12,6},{14,8},{16,10},{18,12},{20,14},{22,16},{... | collective-permute-start | bytes 6291464 | tf_op jit(solution)/shard_map/ppermute | solution.py:17
  698.7 92.3 %collective-permute-start.10 = (bf16[512,2048]{0,1:T(8,128)(2,1)}, bf16[512,2048]{0,1:T(8,128)(2,1)}, u32[]{:S(2)}, u32[]{:S(2)}) collective-permute-start(bf16[512,2048]{0,1:T(8,128)(2,1)} %bitcast.55), channel_id=1, source_target_pairs={{4,0},{6,2},{8,4},{10,6},{12,8},{14,10},{16,12},{18,14},{20,16},{2... | collective-permute-start | bytes 6291464 | tf_op jit(solution)/shard_map/ppermute | solution.py:17
  703.1 93.1 %collective-permute-start.9 = (bf16[512,2048]{0,1:T(8,128)(2,1)}, bf16[512,2048]{0,1:T(8,128)(2,1)}, u32[]{:S(2)}, u32[]{:S(2)}) collective-permute-start(bf16[512,2048]{0,1:T(8,128)(2,1)} %bitcast.54), channel_id=1, source_target_pairs={{2,0},{4,2},{6,4},{8,6},{10,8},{12,10},{14,12},{16,14},{18,16},{20... | collective-permute-start | bytes 6291464 | tf_op jit(solution)/shard_map/ppermute | solution.py:17
  708.7 48.3 %all-to-all-start.5 = ((bf16[2,256,2048]{2,1,0:T(8,128)(2,1)}), bf16[2,256,2048]{2,1,0:T(8,128)(2,1)S(1)}, u32[]{:S(2)}, u32[]{:S(2)}) async-start(bf16[2,256,2048]{2,1,0:T(8,128)(2,1)} %all_to_all.126), calls=%async_computation.5 | async-start | bytes 4194304 | tf_op jit(solution)/shard_map/all_to_all | solution.py:217
  718.5 112.4 %collective-permute-start.8 = (bf16[512,2048]{0,1:T(8,128)(2,1)}, bf16[512,2048]{0,1:T(8,128)(2,1)}, u32[]{:S(2)}, u32[]{:S(2)}) collective-permute-start(bf16[512,2048]{0,1:T(8,128)(2,1)} %bitcast.48), channel_id=1, source_target_pairs={{6,0},{8,2},{10,4},{12,6},{14,8},{16,10},{18,12},{20,14},{22,16},{... | collective-permute-start | bytes 6291464 | tf_op jit(solution)/shard_map/ppermute | solution.py:17
  720.7 160.5 %collective-permute-start.7 = (bf16[512,2048]{0,1:T(8,128)(2,1)}, bf16[512,2048]{0,1:T(8,128)(2,1)}, u32[]{:S(2)}, u32[]{:S(2)}) collective-permute-start(bf16[512,2048]{0,1:T(8,128)(2,1)} %bitcast.47), channel_id=1, source_target_pairs={{4,0},{6,2},{8,4},{10,6},{12,8},{14,10},{16,12},{18,14},{20,16},{2... | collective-permute-start | bytes 6291464 | tf_op jit(solution)/shard_map/ppermute | solution.py:17
  741.0 164.9 %collective-permute-start.6 = (bf16[512,2048]{0,1:T(8,128)(2,1)}, bf16[512,2048]{0,1:T(8,128)(2,1)}, u32[]{:S(2)}, u32[]{:S(2)}) collective-permute-start(bf16[512,2048]{0,1:T(8,128)(2,1)} %bitcast.46), channel_id=1, source_target_pairs={{2,0},{4,2},{6,4},{8,6},{10,8},{12,10},{14,12},{16,14},{18,16},{20... | collective-permute-start | bytes 6291464 | tf_op jit(solution)/shard_map/ppermute | solution.py:17
  757.1 39.1 %copy-start = (bf16[2,256,2048]{2,1,0:T(8,128)(2,1)}, bf16[2,256,2048]{2,1,0:T(8,128)(2,1)S(1)}, u32[]{:S(2)}) copy-start(bf16[2,256,2048]{2,1,0:T(8,128)(2,1)S(1)} %all-to-all-done.5) | copy-start | bytes 6291460
  757.1 46.1 %all-to-all-start.3 = ((bf16[2,256,2048]{2,1,0:T(8,128)(2,1)}), bf16[2,256,2048]{2,1,0:T(8,128)(2,1)}, u32[]{:S(2)}, u32[]{:S(2)}) async-start(bf16[2,256,2048]{2,1,0:T(8,128)(2,1)} %all_to_all.119), calls=%async_computation.3 | async-start | bytes 4194304 | tf_op jit(solution)/shard_map/all_to_all | solution.py:184
  803.2 109.7 %all-to-all-start.7 = ((bf16[2,256,2048]{2,1,0:T(8,128)(2,1)}), bf16[2,256,2048]{2,1,0:T(8,128)(2,1)}, u32[]{:S(2)}, u32[]{:S(2)}) async-start(bf16[2,256,2048]{2,1,0:T(8,128)(2,1)} %bitcast.205), calls=%async_computation.7 | async-start | bytes 4194304 | tf_op jit(solution)/shard_map/all_to_all | solution.py:221
  912.9 22.9 %all-to-all-start.6 = ((bf16[2,256,2048]{2,1,0:T(8,128)(2,1)}), bf16[2,256,2048]{2,1,0:T(8,128)(2,1)}, u32[]{:S(2)}, u32[]{:S(2)}) async-start(bf16[2,256,2048]{2,1,0:T(8,128)(2,1)} %bitcast.206), calls=%async_computation.6 | async-start | bytes 4194304 | tf_op jit(solution)/shard_map/all_to_all | solution.py:218
  (3 other events, 21.4 us)
where the time goes:
time: 953 us; the launch traced here: 942 us
  waiting for transfers between devices  335 us (35%)
  matrix products  286 us (30%)
  local copies, waits for them, and re-layouts  173 us (18%)
  starting transfers between devices  85.6 us (9%)
  other arithmetic  59.8 us (6%)
    ppermute x12, waiting for transfers between devices, shifted(): return lax.ppermute(shard, axis, pairs)  296 us
    dot_general x32, matrix products, masked_scores(): jnp.einsum('be,kce->bkc', query_head, keys_head, preferred_element_type=j...  64.2 us
    ppermute x12, starting transfers between devices, shifted(): return lax.ppermute(shard, axis, pairs)  45.2 us
    unnamed x25, local copies, waits for them, and re-layouts  43.2 us
    dot_general x16, matrix products, forward_one_head(): jnp.einsum('bkc,kce->be', probs_low, values_head, preferred_element_type=...  36.9 us
    dot_general x16, matrix products, backward_one_head(): jnp.einsum('bkc,kce->be', score_grad, keys_head, preferred_element_type=j...  35.6 us
    dynamic_slice x32, local copies, waits for them, and re-layouts, forward_heads(): lax.map(forward_one_head, (jnp.swapaxes(query_block, 0, 1), keys_chosen,...  33.3 us
    dynamic_update_slice x48, local copies, waits for them, and re-layouts, backward_heads(): lax.map(backward_one_head, (jnp.swapaxes(query_block, 0, 1), jnp.swapaxes...  27.7 us
  transfers between devices with their start and end apart: 20, of which 14 were waited for; matrix products, arithmetic and copies ran while one was open for 12% of the time, Pallas kernels for 0%

commit v1 on v0

v1 whole, which is shorter than its diff:
```python
import functools
import jax
import jax.numpy as jnp
from jax import lax
from jax.experimental import pallas as pl
from jax.experimental.pallas import tpu as pltpu
from jax.sharding import PartitionSpec as P

HEAD_DIM = 128
BLOCK = 512
REACH = 3
NEGATIVE = -1e30
CHUNKS = 2


def nt(a, b):
    return lax.dot_general(a, b, (((1,), (1,)), ((), ())), preferred_element_type=jnp.float32)


def nn(a, b):
    return lax.dot_general(a, b, (((1,), (0,)), ((), ())), preferred_element_type=jnp.float32)


def one_head(q, g, keys, values, biases):
    scale = HEAD_DIM**-0.5
    scores = [nt(k, q) * scale + b for k, b in zip(keys, biases)]
    top = functools.reduce(
        jnp.maximum, [jnp.max(s, axis=0, keepdims=True) for s in scores]
    )
    exps = [jnp.exp(s - top) for s in scores]
    total = functools.reduce(jnp.add, [jnp.sum(e, axis=0, keepdims=True) for e in exps])
    inverse = 1.0 / total
    probs = [e * inverse for e in exps]
    lows = [p.astype(jnp.bfloat16) for p in probs]
    out_t = functools.reduce(
        jnp.add, [nn(v.T, p) for v, p in zip(values, lows)]
    )
    out_low = out_t.astype(jnp.bfloat16)
    g_t = g.astype(jnp.float32).T
    delta = jnp.sum(out_low.astype(jnp.float32) * g_t, axis=0, keepdims=True)
    grads = [
        (p * (nt(v, g) - delta)).astype(jnp.bfloat16) for p, v in zip(probs, values)
    ]
    dq_t = functools.reduce(jnp.add, [nn(k.T, d) for k, d in zip(keys, grads)]) * scale
    dks = [nn(d, q) * scale for d in grads]
    dvs = [nn(p, g) for p in lows]
    return out_t.T.astype(jnp.bfloat16), dq_t.T.astype(jnp.bfloat16), dks, dvs


def attend(slots, docs_q, docs_k, qg, own, near, mid, far, out, parts, bias):
    i = pl.program_id(0)

    @pl.when(i == 0)
    def _():
        rows = lax.broadcasted_iota(jnp.int32, (BLOCK, BLOCK), 0)
        cols = lax.broadcasted_iota(jnp.int32, (BLOCK, BLOCK), 1)
        for w in range(4):
            ok = docs_k[w] == docs_q[...]
            if w == 3:
                ok = jnp.logical_and(ok, rows <= cols)
            bias[w] = jnp.where(ok, 0.0, NEGATIVE)

    a, b = slots[0, i], slots[1, i]

    def pick(n, which):
        return jnp.where(n == 0, near[which], jnp.where(n == 1, mid[which], far[which]))

    keys = [pick(a, 0), pick(b, 0), own[0]]
    values = [pick(a, 1), pick(b, 1), own[1]]
    biases = [bias[a], bias[b], bias[3]]
    o, dq, dks, dvs = one_head(qg[0], qg[1], keys, values, biases)
    out[0] = o
    out[1] = dq
    for which, d in ((0, dks), (1, dvs)):
        parts[3, which] = d[2].astype(jnp.bfloat16)
        for w in range(3):
            here = jnp.where(a == w, d[0], jnp.where(b == w, d[1], 0.0))
            parts[w, which] = here.astype(jnp.bfloat16)


def attention(slots, docs_q, docs_k, qg, own, near, mid, far):
    heads = qg.shape[2] // HEAD_DIM
    pair = pl.BlockSpec((2, BLOCK, HEAD_DIM), lambda i, *_: (0, 0, i))
    width = qg.shape[2]
    return pl.pallas_call(
        attend,
        grid_spec=pltpu.PrefetchScalarGridSpec(
            num_scalar_prefetch=1,
            grid=(heads,),
            in_specs=[
                pl.BlockSpec((1, BLOCK), lambda i, *_: (0, 0)),
                pl.BlockSpec((4, BLOCK, 1), lambda i, *_: (0, 0, 0)),
                pair,
                pair,
                pair,
                pair,
                pair,
            ],
            out_specs=[
                pair,
                pl.BlockSpec((4, 2, BLOCK, HEAD_DIM), lambda i, *_: (0, 0, 0, i)),
            ],
            scratch_shapes=[pltpu.VMEM((4, BLOCK, BLOCK), jnp.float32)],
        ),
        out_shape=[
            jax.ShapeDtypeStruct((2, BLOCK, width), jnp.bfloat16),
            jax.ShapeDtypeStruct((4, 2, BLOCK, width), jnp.bfloat16),
        ],
        compiler_params=pltpu.CompilerParams(
            dimension_semantics=("arbitrary",), vmem_limit_bytes=50 * 2**20
        ),
        cost_estimate=pl.CostEstimate(
            flops=heads * 12 * 128 * 512 * 1536 * 3,
            bytes_accessed=20 * BLOCK * width * 2,
            transcendentals=heads * 512 * 1536,
        ),
    )(slots, docs_q, docs_k, qg, own, near, mid, far)


def per_device(queries, key_rows, value_rows, out_grad, doc_ids, picks):
    peers = lax.axis_size("head")
    length = lax.axis_size("seq")
    seq = lax.axis_index("seq")
    rank = lax.axis_index("head")
    rows = queries.shape[0]
    width = queries.shape[1] // peers
    heads = width // HEAD_DIM
    chunks = CHUNKS
    part = width // chunks

    def gather_heads(arrays, c):
        x = jnp.stack(arrays)

        if peers != 2:
            x = x.reshape(2, rows, peers, width)[..., c * part : (c + 1) * part]
            x = lax.all_to_all(x, "head", split_axis=2, concat_axis=1, tiled=True)
            return x.reshape(2, rows * peers, part)

        def columns(r):
            return lax.dynamic_slice_in_dim(x, r * width + c * part, part, 2)

        mine = columns(rank)
        theirs = lax.ppermute(columns(1 - rank), "head", [(0, 1), (1, 0)])
        return jnp.where(
            rank == 0,
            jnp.concatenate([mine, theirs], axis=1),
            jnp.concatenate([theirs, mine], axis=1),
        )

    def give_tokens(x):
        if peers != 2:
            x = lax.all_to_all(x, "head", split_axis=1, concat_axis=2, tiled=True)
            return x.reshape(2, rows, peers, part)

        def tokens(r):
            return lax.dynamic_slice_in_dim(x, r * rows, rows, 1)

        mine = tokens(rank)
        theirs = lax.ppermute(tokens(1 - rank), "head", [(0, 1), (1, 0)])
        return jnp.where(
            rank == 0,
            jnp.stack([mine, theirs], axis=2),
            jnp.stack([theirs, mine], axis=2),
        )

    def inside(pairs):
        return [(a, b) for a, b in pairs if 0 <= a < length and 0 <= b < length]

    two = inside([(s, s + 2) for s in range(length)])
    odd = inside([(s, s + 1 if s % 2 == 0 else s + 3) for s in range(length)])
    mate = inside([(s, s ^ 1) for s in range(length)])

    def back(pairs):
        return [(b, a) for a, b in pairs]

    parity = seq % 2
    local = picks[0].T
    slots = jnp.where(local == 2, 1, jnp.where((local == 1) == (parity == 1), 0, 2))
    offsets = jnp.stack(
        [jnp.where(parity == 1, 1, 3), jnp.int32(2), jnp.where(parity == 1, 3, 1), jnp.int32(0)]
    )
    docs_pad = jnp.concatenate([jnp.full((REACH * BLOCK,), -1, jnp.int32), doc_ids])
    starts = (seq + REACH - offsets) * BLOCK
    docs_k = jnp.stack(
        [lax.dynamic_slice_in_dim(docs_pad, starts[w], BLOCK, 0) for w in range(4)]
    )
    docs_q = docs_k[3:4]
    docs_k = docs_k[:, :, None]

    per = heads // chunks
    outs, grads = [], []
    for c in range(chunks):
        own = gather_heads([key_rows, value_rows], c)
        qg = gather_heads([queries, out_grad], c)
        near = lax.ppermute(own, "seq", odd)
        mid = lax.ppermute(own, "seq", two)
        far = lax.ppermute(mid, "seq", mate)
        out, parts = attention(
            slots[:, c * per : (c + 1) * per], docs_q, docs_k, qg, own, near, mid, far
        )
        outs.append(give_tokens(out))
        swapped = lax.ppermute(parts[2], "seq", back(mate))
        from_near = lax.ppermute(parts[0], "seq", back(odd))
        joined = (parts[1].astype(jnp.float32) + swapped.astype(jnp.float32)).astype(jnp.bfloat16)
        from_mid = lax.ppermute(joined, "seq", back(two))
        total = (
            parts[3].astype(jnp.float32)
            + from_near.astype(jnp.float32)
            + from_mid.astype(jnp.float32)
        ).astype(jnp.bfloat16)
        grads.append(give_tokens(total))

    def whole(pieces, which):
        x = jnp.stack([p[which] for p in pieces], axis=2)
        return x.reshape(rows, peers * width)

    return (whole(outs, 0), whole(outs, 1), whole(grads, 0), whole(grads, 1))


def solution(mesh):
    tokens = P(("seq", "head"), None)
    return jax.shard_map(
        per_device,
        mesh=mesh,
        in_specs=(tokens, tokens, tokens, tokens, P(), P("seq", "head", None)),
        out_specs=(tokens, tokens, tokens, tokens),
        check_vma=False,
    )
```

time: 953 us -> 407 us (0.43)
  the two profiles are of different devices: /device:TPU:23 before, /device:TPU:20 now
where the time goes in v1:
time: 407 us; the launch traced here: 406 us
  waiting for transfers between devices  217 us (53%)
  Pallas kernels  60.4 us (15%)
  local copies, waits for them, and re-layouts  46.2 us (11%)
  other arithmetic  42.1 us (10%)
  starting transfers between devices  32.3 us (8%)
  between operations  7.99 us (2%)
    ppermute x2, waiting for transfers between devices, per_device(): from_mid = lax.ppermute(joined, 'seq', back(two))  97 us
    ppermute x4, waiting for transfers between devices, gather_heads(): theirs = lax.ppermute(columns(1 - rank), 'head', [(0, 1), (1, 0)])  77.9 us
    pallas_call x2, Pallas kernels, attention(): pl.pallas_call(attend, grid_spec=pltpu.PrefetchScalarGridSpec(num_scalar_...  60.4 us
    unnamed x22, local copies, waits for them, and re-layouts  18.8 us
    ppermute x2, waiting for transfers between devices, per_device(): mid = lax.ppermute(own, 'seq', two)  15.8 us
    another operation x8, local copies, waits for them, and re-layouts, whole(): x = jnp.stack([p[which] for p in pieces], axis=2)  15.1 us
    select_n x4, other arithmetic, gather_heads(): jnp.where(rank == 0, jnp.concatenate([mine, theirs], axis=1), jnp.concate...  14 us
    ppermute x2, waiting for transfers between devices, per_device(): near = lax.ppermute(own, 'seq', odd)  11.2 us
  transfers between devices with their start and end apart: 20, of which 10 were waited for; matrix products, arithmetic and copies ran while one was open for 11% of the time, Pallas kernels for 15%

profile of v1, /device:TPU:20, one launch (start us, length us, event | category | flops | bytes accessed | tf_op | source)
XLA Modules:
  0.0 405.8 jit_solution(9983876716932016653)
XLA Ops:
  6.0 23.7 %collective-permute-done.7 = bf16[2,256,1024]{2,1,0:T(8,128)(2,1)} collective-permute-done((bf16[2,256,1024]{2,1,0:T(8,128)(2,1)}, bf16[2,256,1024]{2,1,0:T(8,128)(2,1)}, u32[]{:S(2)}, u32[]{:S(2)}) %collective-permute-start.7) | collective-permute-done | bytes 1048608 | tf_op jit(solution)/shard_map/ppermute | solution.py:143
  29.7 3.9 maximum_select_fusion.4.own
  38.6 22.3 %collective-permute-done.1 = bf16[2,256,1024]{2,1,0:T(8,128)(2,1)S(1)} collective-permute-done((bf16[2,256,1024]{2,1,0:T(8,128)(2,1)S(1)}, bf16[2,256,1024]{2,1,0:T(8,128)(2,1)S(1)}, u32[]{:S(2)}, u32[]{:S(2)}) %collective-permute-start.1) | collective-permute-done | bytes 1048608 | tf_op jit(solution)/shard_map/ppermute | solution.py:143
  68.5 15.8 %collective-permute-done.9.mid = bf16[2,512,1024]{2,1,0:T(8,128)(2,1)} collective-permute-done((bf16[2,512,1024]{2,1,0:T(8,128)(2,1)}, bf16[2,512,1024]{2,1,0:T(8,128)(2,1)}, u32[]{:S(2)}, u32[]{:S(2)}) %collective-permute-start.9) | collective-permute-done | bytes 2097184 | tf_op jit(solution)/shard_map/ppermute | solution.py:196
  96.6 15.8 %collective-permute-done.6 = bf16[2,256,1024]{2,1,0:T(8,128)(2,1)} collective-permute-done((bf16[2,256,1024]{2,1,0:T(8,128)(2,1)}, bf16[2,256,1024]{2,1,0:T(8,128)(2,1)}, u32[]{:S(2)}, u32[]{:S(2)}) %collective-permute-start.6) | collective-permute-done | bytes 1048608 | tf_op jit(solution)/shard_map/ppermute | solution.py:143
  118.4 16.1 %collective-permute-done = bf16[2,256,1024]{2,1,0:T(8,128)(2,1)} collective-permute-done((bf16[2,256,1024]{2,1,0:T(8,128)(2,1)}, bf16[2,256,1024]{2,1,0:T(8,128)(2,1)}, u32[]{:S(2)}, u32[]{:S(2)}) %collective-permute-start) | collective-permute-done | bytes 1048608 | tf_op jit(solution)/shard_map/ppermute | solution.py:143
  134.5 3.9 maximum_select_fusion.qg
  138.4 11.2 %collective-permute-done.8.near = bf16[2,512,1024]{2,1,0:T(8,128)(2,1)} collective-permute-done((bf16[2,512,1024]{2,1,0:T(8,128)(2,1)}, bf16[2,512,1024]{2,1,0:T(8,128)(2,1)}, u32[]{:S(2)}, u32[]{:S(2)}) %collective-permute-start.8) | collective-permute-done | bytes 2097184 | tf_op jit(solution)/shard_map/ppermute | solution.py:195
  149.6 30.2 %shard_map.94 = (bf16[2,512,1024]{2,1,0:T(8,128)(2,1)S(1)}, bf16[4,2,512,1024]{3,2,1,0:T(8,128)(2,1)}) custom-call(s32[2,8]{1,0:T(2,128)S(1)} %get-tuple-element.49.slots, s32[1,512]{1,0:T(1,128)S(1)} %bitcast.75, s32[4,512,1]{2,1,0:T(8,128)S(1)} %copy.12.docs_k, bf16[2,512,1024]{2,1,0:T(8,128)(2,1)} %maximum_select_fusion.3.qg, ...), custom_call_target="tpu_custom_call" | custom-call | flops 28991029248 | bytes 20971520 | tf_op jit(solution)/shard_map/pallas_call | solution.py:85
  179.8 4.1 slice_bitcast_fusion.1
  185.9 30.2 %shard_map.93 = (bf16[2,512,1024]{2,1,0:T(8,128)(2,1)S(1)}, bf16[4,2,512,1024]{3,2,1,0:T(8,128)(2,1)}) custom-call(s32[2,8]{1,0:T(2,128)S(1)} %get-tuple-element.48.slots, s32[1,512]{1,0:T(1,128)S(1)} %bitcast.76, s32[4,512,1]{2,1,0:T(8,128)S(1)} %copy.12.docs_k, bf16[2,512,1024]{2,1,0:T(8,128)(2,1)} %maximum_select_fusion.qg, ...), custom_call_target="tpu_custom_call" | custom-call | flops 28991029248 | bytes 20971520 | tf_op jit(solution)/shard_map/pallas_call | solution.py:85
  216.1 4.8 %slice_bitcast_fusion.3 = (bf16[2,512,1024]{2,1,0:T(8,128)(2,1)}, bf16[2,512,1024]{2,1,0:T(8,128)(2,1)S(1)}) fusion(bf16[4,2,512,1024]{3,2,1,0:T(8,128)(2,1)} %get-tuple-element.10), kind=kLoop, calls=%fused_computation.41 | loop fusion | bytes 8388608 | tf_op jit(solution)/shard_map/squeeze | solution.py:203
  223.4 3.9 fusion
  231.8 3.9 fusion.3
  242.5 4.7 %collective-permute-done.16 = bf16[2,512,1024]{2,1,0:T(8,128)(2,1)} collective-permute-done((bf16[2,512,1024]{2,1,0:T(8,128)(2,1)}, bf16[2,512,1024]{2,1,0:T(8,128)(2,1)}, u32[]{:S(2)}, u32[]{:S(2)}) %collective-permute-start.16) | collective-permute-done | bytes 2097184 | tf_op jit(solution)/shard_map/ppermute | solution.py:203
  248.7 41.5 %collective-permute-done.18 = bf16[2,512,1024]{2,1,0:T(8,128)(2,1)} collective-permute-done((bf16[2,512,1024]{2,1,0:T(8,128)(2,1)}, bf16[2,512,1024]{2,1,0:T(8,128)(2,1)}, u32[]{:S(2)}, u32[]{:S(2)}) %collective-permute-start.18) | collective-permute-done | bytes 2097184 | tf_op jit(solution)/shard_map/ppermute | solution.py:205
  290.2 4.3 %fusion.2 = bf16[2,512,1024]{2,1,0:T(8,128)(2,1)S(1)} fusion(bf16[2,512,1024]{2,1,0:T(8,128)(2,1)} %collective-permute-done.18, bf16[2,512,1024]{2,1,0:T(8,128)(2,1)} %collective-permute-done.16, bf16[4,2,512,1024]{3,2,1,0:T(8,128)(2,1)} %get-tuple-element.11), kind=kLoop, calls=%fused_computation.20 | loop fusion | flops 6291456 | bytes 8388608 | tf_op jit(solution)/shard_map/convert_element_type | solution.py:210
  296.3 55.4 %collective-permute-done.14 = bf16[2,512,1024]{2,1,0:T(8,128)(2,1)} collective-permute-done((bf16[2,512,1024]{2,1,0:T(8,128)(2,1)}, bf16[2,512,1024]{2,1,0:T(8,128)(2,1)}, u32[]{:S(2)}, u32[]{:S(2)}) %collective-permute-start.14) | collective-permute-done | bytes 2097184 | tf_op jit(solution)/shard_map/ppermute | solution.py:205
  351.7 4.3 %fusion.5 = bf16[2,512,1024]{2,1,0:T(8,128)(2,1)S(1)} fusion(bf16[2,512,1024]{2,1,0:T(8,128)(2,1)} %collective-permute-done.14, bf16[2,512,1024]{2,1,0:T(8,128)(2,1)} %collective-permute-done.12, bf16[4,2,512,1024]{3,2,1,0:T(8,128)(2,1)} %get-tuple-element.10), kind=kLoop, calls=%fused_computation.25 | loop fusion | flops 6291456 | bytes 8388608 | tf_op jit(solution)/shard_map/convert_element_type | solution.py:210
  361.0 10.1 %collective-permute-done.15 = bf16[2,256,1024]{2,1,0:T(8,128)(2,1)S(1)} collective-permute-done((bf16[2,256,1024]{2,1,0:T(8,128)(2,1)S(1)}, bf16[2,256,1024]{2,1,0:T(8,128)(2,1)S(1)}, u32[]{:S(2)}, u32[]{:S(2)}) %collective-permute-start.15) | collective-permute-done | bytes 1048608 | tf_op jit(solution)/shard_map/ppermute | solution.py:159
  376.8 4.1 %copy.23 = bf16[256,4096]{1,0:T(8,128)(2,1)} copy(bf16[256,4096]{0,1:T(8,128)(2,1)} %bitcast.77) | data formatting | bytes 4194304
  385.2 4.2 %copy.22 = bf16[256,4096]{1,0:T(8,128)(2,1)} copy(bf16[256,4096]{0,1:T(8,128)(2,1)} %bitcast.78) | data formatting | bytes 4194304
  393.7 4.1 %copy.21 = bf16[256,4096]{1,0:T(8,128)(2,1)} copy(bf16[256,4096]{0,1:T(8,128)(2,1)} %bitcast.79) | data formatting | bytes 4194304
  401.8 4.1 %copy.20 = bf16[256,4096]{1,0:T(8,128)(2,1)} copy(bf16[256,4096]{0,1:T(8,128)(2,1)} %bitcast.80) | data formatting | bytes 4194304
  (78 shorter events, 71.3 us)
Async XLA Ops:
  4.5 25.2 %collective-permute-start.7 = (bf16[2,256,1024]{2,1,0:T(8,128)(2,1)}, bf16[2,256,1024]{2,1,0:T(8,128)(2,1)}, u32[]{:S(2)}, u32[]{:S(2)}) collective-permute-start(bf16[2,256,1024]{2,1,0:T(8,128)(2,1)} %get-tuple-element.23), channel_id=1, source_target_pairs={{0,1},{1,0},{2,3},{3,2},{4,5},{5,4},{6,7},{7,6},{8,9},{9,8},{10,11... | collective-permute-start | bytes 3145736 | tf_op jit(solution)/shard_map/ppermute | solution.py:143
  33.6 50.8 %collective-permute-start.9 = (bf16[2,512,1024]{2,1,0:T(8,128)(2,1)}, bf16[2,512,1024]{2,1,0:T(8,128)(2,1)}, u32[]{:S(2)}, u32[]{:S(2)}) collective-permute-start(bf16[2,512,1024]{2,1,0:T(8,128)(2,1)} %maximum_select_fusion.4.own), channel_id=1, source_target_pairs={{0,4},{2,6},{4,8},{6,10},{8,12},{10,14},{12,16},{14,18},{16,20},{1... | collective-permute-start | bytes 6291464 | tf_op jit(solution)/shard_map/ppermute | solution.py:196
  37.0 23.8 %collective-permute-start.1 = (bf16[2,256,1024]{2,1,0:T(8,128)(2,1)S(1)}, bf16[2,256,1024]{2,1,0:T(8,128)(2,1)S(1)}, u32[]{:S(2)}, u32[]{:S(2)}) collective-permute-start(bf16[2,256,1024]{2,1,0:T(8,128)(2,1)S(1)} %get-tuple-element.21), channel_id=1, source_target_pairs={{0,1},{1,0},{2,3},{3,2},{4,5},{5,4},{6,7},{7,6},{8,9},{9,8},{10,11... | collective-permute-start | bytes 3145736 | tf_op jit(solution)/shard_map/ppermute | solution.py:143
  60.8 23.5 %copy-start.3 = (bf16[256,4096]{1,0:T(8,128)(2,1)S(1)}, bf16[256,4096]{1,0:T(8,128)(2,1)}, u32[]{:S(2)}) copy-start(bf16[256,4096]{1,0:T(8,128)(2,1)} %param.6) | copy-start | bytes 6291460
  60.8 23.5 %copy-start.4 = (bf16[256,4096]{1,0:T(8,128)(2,1)S(1)}, bf16[256,4096]{1,0:T(8,128)(2,1)}, u32[]{:S(2)}) copy-start(bf16[256,4096]{1,0:T(8,128)(2,1)} %param.9) | copy-start | bytes 6291460
  63.2 75.3 %collective-permute-start.3 = (bf16[2,512,1024]{2,1,0:T(8,128)(2,1)}, bf16[2,512,1024]{2,1,0:T(8,128)(2,1)}, u32[]{:S(2)}, u32[]{:S(2)}) collective-permute-start(bf16[2,512,1024]{2,1,0:T(8,128)(2,1)} %maximum_select_fusion.1.own), channel_id=1, source_target_pairs={{0,4},{2,6},{4,8},{6,10},{8,12},{10,14},{12,16},{14,18},{16,20},{1... | collective-permute-start | bytes 6291464 | tf_op jit(solution)/shard_map/ppermute | solution.py:196
  66.6 83.1 %collective-permute-start.8 = (bf16[2,512,1024]{2,1,0:T(8,128)(2,1)}, bf16[2,512,1024]{2,1,0:T(8,128)(2,1)}, u32[]{:S(2)}, u32[]{:S(2)}) collective-permute-start(bf16[2,512,1024]{2,1,0:T(8,128)(2,1)} %maximum_select_fusion.4.own), channel_id=1, source_target_pairs={{0,2},{2,8},{4,6},{6,12},{8,10},{10,16},{12,14},{14,20},{16,18},{1... | collective-permute-start | bytes 6291464 | tf_op jit(solution)/shard_map/ppermute | solution.py:195
  84.3 65.3 %collective-permute-start.10 = (bf16[2,512,1024]{2,1,0:T(8,128)(2,1)}, bf16[2,512,1024]{2,1,0:T(8,128)(2,1)}, u32[]{:S(2)}, u32[]{:S(2)}) collective-permute-start(bf16[2,512,1024]{2,1,0:T(8,128)(2,1)} %collective-permute-done.9.mid), channel_id=1, source_target_pairs={{0,2},{2,0},{4,6},{6,4},{8,10},{10,8},{12,14},{14,12},{16,18},{18,... | collective-permute-start | bytes 6291464 | tf_op jit(solution)/shard_map/ppermute | solution.py:197
  84.4 11.7 %copy-start.5 = (s32[8192]{0:T(1024)S(1)}, s32[8192]{0:T(1024)}, u32[]{:S(2)}) copy-start(s32[8192]{0:T(1024)} %param.10) | copy-start | bytes 98308
  84.4 12.2 %copy-start.6 = (s32[1,16,2]{1,2,0:T(2,128)S(1)}, s32[1,16,2]{1,2,0:T(2,128)}, u32[]{:S(2)}) copy-start(s32[1,16,2]{1,2,0:T(2,128)} %param.11) | copy-start | bytes 388
  86.2 26.3 %collective-permute-start.6 = (bf16[2,256,1024]{2,1,0:T(8,128)(2,1)}, bf16[2,256,1024]{2,1,0:T(8,128)(2,1)}, u32[]{:S(2)}, u32[]{:S(2)}) collective-permute-start(bf16[2,256,1024]{2,1,0:T(8,128)(2,1)} %get-tuple-element.27), channel_id=1, source_target_pairs={{0,1},{1,0},{2,3},{3,2},{4,5},{5,4},{6,7},{7,6},{8,9},{9,8},{10,11... | collective-permute-start | bytes 3145736 | tf_op jit(solution)/shard_map/ppermute | solution.py:143
  87.7 46.8 %collective-permute-start = (bf16[2,256,1024]{2,1,0:T(8,128)(2,1)}, bf16[2,256,1024]{2,1,0:T(8,128)(2,1)}, u32[]{:S(2)}, u32[]{:S(2)}) collective-permute-start(bf16[2,256,1024]{2,1,0:T(8,128)(2,1)} %get-tuple-element.25), channel_id=1, source_target_pairs={{0,1},{1,0},{2,3},{3,2},{4,5},{5,4},{6,7},{7,6},{8,9},{9,8},{10,11... | collective-permute-start | bytes 3145736 | tf_op jit(solution)/shard_map/ppermute | solution.py:143
  112.4 71.4 %collective-permute-start.2 = (bf16[2,512,1024]{2,1,0:T(8,128)(2,1)}, bf16[2,512,1024]{2,1,0:T(8,128)(2,1)S(1)}, u32[]{:S(2)}, u32[]{:S(2)}) collective-permute-start(bf16[2,512,1024]{2,1,0:T(8,128)(2,1)} %maximum_select_fusion.1.own), channel_id=1, source_target_pairs={{0,2},{2,8},{4,6},{6,12},{8,10},{10,16},{12,14},{14,20},{16,18},{1... | collective-permute-start | bytes 6291464 | tf_op jit(solution)/shard_map/ppermute | solution.py:195
  138.4 45.5 %collective-permute-start.4 = (bf16[2,512,1024]{2,1,0:T(8,128)(2,1)}, bf16[2,512,1024]{2,1,0:T(8,128)(2,1)S(1)}, u32[]{:S(2)}, u32[]{:S(2)}) collective-permute-start(bf16[2,512,1024]{2,1,0:T(8,128)(2,1)} %collective-permute-done.3.mid), channel_id=1, source_target_pairs={{0,2},{2,0},{4,6},{6,4},{8,10},{10,8},{12,14},{14,12},{16,18},{18,... | collective-permute-start | bytes 6291464 | tf_op jit(solution)/shard_map/ppermute | solution.py:197
  183.9 39.5 %collective-permute-start.17 = (bf16[2,512,1024]{2,1,0:T(8,128)(2,1)S(1)}, bf16[2,512,1024]{2,1,0:T(8,128)(2,1)S(1)}, u32[]{:S(2)}, u32[]{:S(2)}) collective-permute-start(bf16[2,512,1024]{2,1,0:T(8,128)(2,1)S(1)} %get-tuple-element.19), channel_id=1, source_target_pairs={{2,0},{0,2},{6,4},{4,6},{10,8},{8,10},{14,12},{12,14},{18,16},{16,... | collective-permute-start | bytes 6291464 | tf_op jit(solution)/shard_map/ppermute | solution.py:202
  220.8 11.0 %collective-permute-start.13 = (bf16[2,512,1024]{2,1,0:T(8,128)(2,1)S(1)}, bf16[2,512,1024]{2,1,0:T(8,128)(2,1)S(1)}, u32[]{:S(2)}, u32[]{:S(2)}) collective-permute-start(bf16[2,512,1024]{2,1,0:T(8,128)(2,1)S(1)} %get-tuple-element.17), channel_id=1, source_target_pairs={{2,0},{0,2},{6,4},{4,6},{10,8},{8,10},{14,12},{12,14},{18,16},{16,... | collective-permute-start | bytes 6291464 | tf_op jit(solution)/shard_map/ppermute | solution.py:202
  221.4 25.8 %collective-permute-start.16 = (bf16[2,512,1024]{2,1,0:T(8,128)(2,1)}, bf16[2,512,1024]{2,1,0:T(8,128)(2,1)}, u32[]{:S(2)}, u32[]{:S(2)}) collective-permute-start(bf16[2,512,1024]{2,1,0:T(8,128)(2,1)} %get-tuple-element.18), channel_id=1, source_target_pairs={{2,0},{8,2},{6,4},{12,6},{10,8},{16,10},{14,12},{20,14},{18,16},{2... | collective-permute-start | bytes 6291464 | tf_op jit(solution)/shard_map/ppermute | solution.py:203
  227.3 62.9 %collective-permute-start.18 = (bf16[2,512,1024]{2,1,0:T(8,128)(2,1)}, bf16[2,512,1024]{2,1,0:T(8,128)(2,1)}, u32[]{:S(2)}, u32[]{:S(2)}) collective-permute-start(bf16[2,512,1024]{2,1,0:T(8,128)(2,1)} %fusion), channel_id=1, source_target_pairs={{4,0},{6,2},{8,4},{10,6},{12,8},{14,10},{16,12},{18,14},{20,16},{2... | collective-permute-start | bytes 6291464 | tf_op jit(solution)/shard_map/ppermute | solution.py:205
  229.2 67.1 %collective-permute-start.12 = (bf16[2,512,1024]{2,1,0:T(8,128)(2,1)}, bf16[2,512,1024]{2,1,0:T(8,128)(2,1)}, u32[]{:S(2)}, u32[]{:S(2)}) collective-permute-start(bf16[2,512,1024]{2,1,0:T(8,128)(2,1)} %get-tuple-element.16), channel_id=1, source_target_pairs={{2,0},{8,2},{6,4},{12,6},{10,8},{16,10},{14,12},{20,14},{18,16},{2... | collective-permute-start | bytes 6291464 | tf_op jit(solution)/shard_map/ppermute | solution.py:203
  235.7 116.0 %collective-permute-start.14 = (bf16[2,512,1024]{2,1,0:T(8,128)(2,1)}, bf16[2,512,1024]{2,1,0:T(8,128)(2,1)}, u32[]{:S(2)}, u32[]{:S(2)}) collective-permute-start(bf16[2,512,1024]{2,1,0:T(8,128)(2,1)} %fusion.3), channel_id=1, source_target_pairs={{4,0},{6,2},{8,4},{10,6},{12,8},{14,10},{16,12},{18,14},{20,16},{2... | collective-permute-start | bytes 6291464 | tf_op jit(solution)/shard_map/ppermute | solution.py:205
  240.7 120.2 %collective-permute-start.5 = (bf16[2,256,1024]{2,1,0:T(8,128)(2,1)S(1)}, bf16[2,256,1024]{2,1,0:T(8,128)(2,1)S(1)}, u32[]{:S(2)}, u32[]{:S(2)}) collective-permute-start(bf16[2,256,1024]{2,1,0:T(8,128)(2,1)S(1)} %get-tuple-element.41), channel_id=1, source_target_pairs={{0,1},{1,0},{2,3},{3,2},{4,5},{5,4},{6,7},{7,6},{8,9},{9,8},{10,11... | collective-permute-start | bytes 3145736 | tf_op jit(solution)/shard_map/ppermute | solution.py:159
  247.2 110.6 %collective-permute-start.11 = (bf16[2,256,1024]{2,1,0:T(8,128)(2,1)S(1)}, bf16[2,256,1024]{2,1,0:T(8,128)(2,1)S(1)}, u32[]{:S(2)}, u32[]{:S(2)}) collective-permute-start(bf16[2,256,1024]{2,1,0:T(8,128)(2,1)S(1)} %get-tuple-element.43), channel_id=1, source_target_pairs={{0,1},{1,0},{2,3},{3,2},{4,5},{5,4},{6,7},{7,6},{8,9},{9,8},{10,11... | collective-permute-start | bytes 3145736 | tf_op jit(solution)/shard_map/ppermute | solution.py:159
  294.7 64.7 %collective-permute-start.19 = (bf16[2,256,1024]{2,1,0:T(8,128)(2,1)S(1)}, bf16[2,256,1024]{2,1,0:T(8,128)(2,1)S(1)}, u32[]{:S(2)}, u32[]{:S(2)}) collective-permute-start(bf16[2,256,1024]{2,1,0:T(8,128)(2,1)S(1)} %get-tuple-element.35), channel_id=1, source_target_pairs={{0,1},{1,0},{2,3},{3,2},{4,5},{5,4},{6,7},{7,6},{8,9},{9,8},{10,11... | collective-permute-start | bytes 3145736 | tf_op jit(solution)/shard_map/ppermute | solution.py:159
  356.2 14.9 %collective-permute-start.15 = (bf16[2,256,1024]{2,1,0:T(8,128)(2,1)S(1)}, bf16[2,256,1024]{2,1,0:T(8,128)(2,1)S(1)}, u32[]{:S(2)}, u32[]{:S(2)}) collective-permute-start(bf16[2,256,1024]{2,1,0:T(8,128)(2,1)S(1)} %get-tuple-element.33), channel_id=1, source_target_pairs={{0,1},{1,0},{2,3},{3,2},{4,5},{5,4},{6,7},{7,6},{8,9},{9,8},{10,11... | collective-permute-start | bytes 3145736 | tf_op jit(solution)/shard_map/ppermute | solution.py:159
  (5 other events, 13.8 us)

commit v2 on v1

--- a/solution.py
+++ b/solution.py
@@ -11,6 +11,8 @@
 REACH = 3
 NEGATIVE = -1e30
 CHUNKS = 2
+AHEAD = 2
+LAGS = (2, 3, 4, 6)
 
 
 def nt(a, b):
@@ -117,6 +119,323 @@
     )(slots, docs_q, docs_k, qg, own, near, mid, far)
 
 
+def whole_pass(peers, length, slots, docs_q, docs_k, q_ref, k_ref, v_ref, g_ref,
+               o_out, dq_out, dk_out, dv_out,
+               own, near, mid, far, mate_back, near_back, mid_back, bias,
+               in_send, in_recv, in_local, near_send, near_recv, mid_send, mid_recv,
+               far_send, far_recv, back_send, mate_back_recv, near_back_recv, mid_back_recv,
+               out_send, out_recv, out_local):
+    seq = lax.axis_index("seq")
+    rank = lax.axis_index("head")
+    other = 1 - rank
+    heads = own.shape[0]
+    rows = q_ref.shape[0]
+    width = heads * HEAD_DIM
+    parity = lax.rem(seq, 2)
+    even = parity == 0
+    mate = seq + 1 - 2 * parity
+    has_before = seq >= 2
+    has_after = seq + 2 < length
+    near_to = jnp.where(even, seq + 1, seq + 3)
+    near_from = jnp.where(even, seq - 3, seq - 1)
+    near_goes = near_to < length
+    near_comes = near_from >= 0
+    sources = (k_ref, v_ref, q_ref, g_ref)
+    results = (dk_out, dv_out, o_out, dq_out)
+
+    def copy(src, dst, send, recv, where):
+        return pltpu.make_async_remote_copy(
+            src_ref=src, dst_ref=dst, send_sem=send, recv_sem=recv,
+            device_id=where, device_id_type=pl.DeviceIdType.MESH,
+        )
+
+    def token_rows(r):
+        return pl.ds(pl.multiple_of(r * rows, rows), rows)
+
+    def columns(r, g):
+        return pl.ds(pl.multiple_of(r * width + g * HEAD_DIM, HEAD_DIM), HEAD_DIM)
+
+    def group(r):
+        return pl.ds(pl.multiple_of(r * width, width), width)
+
+    def in_copy(a, g):
+        return copy(sources[a].at[:, columns(other, g)], own.at[g, a, token_rows(rank), :],
+                    in_send.at[a], in_recv.at[a, g], (seq, other))
+
+    def in_arrival(a, g):
+        return copy(sources[a].at[:, columns(other, g)], own.at[g, a, token_rows(other), :],
+                    in_send.at[a], in_recv.at[a, g], (seq, other))
+
+    def in_stay(a, g):
+        return pltpu.make_async_copy(sources[a].at[:, columns(rank, g)],
+                                     own.at[g, a, token_rows(rank), :], in_local.at[a, g])
+
+    def near_copy(g):
+        return copy(own.at[g, pl.ds(0, 2)], near.at[g], near_send.at[g], near_recv.at[g],
+                    (near_to, rank))
+
+    def mid_copy(g):
+        return copy(own.at[g, pl.ds(0, 2)], mid.at[g], mid_send.at[g], mid_recv.at[g],
+                    (seq + 2, rank))
+
+    def far_copy(g):
+        return copy(mid.at[g], far.at[g], far_send.at[g], far_recv.at[g], (mate, rank))
+
+    def mate_back_copy(g):
+        return copy(far.at[g], mate_back.at[g], back_send.at[0], mate_back_recv.at[g],
+                    (mate, rank))
+
+    def near_back_copy(g):
+        return copy(near.at[g], near_back.at[g], back_send.at[1], near_back_recv.at[g],
+                    (near_from, rank))
+
+    def mid_back_copy(g):
+        return copy(mid.at[g], mid_back.at[g], back_send.at[2], mid_back_recv.at[g],
+                    (seq - 2, rank))
+
+    def out_copy(a, g):
+        return copy(own.at[g, a, token_rows(other), :], results[a].at[:, columns(rank, g)],
+                    out_send.at[a], out_recv.at[a], (seq, other))
+
+    def out_stay(a, g):
+        return pltpu.make_async_copy(own.at[g, a, token_rows(rank), :],
+                                     results[a].at[:, columns(rank, g)], out_local.at[a])
+
+    barrier = pltpu.get_barrier_semaphore()
+
+    def greet(where):
+        pl.semaphore_signal(barrier, inc=1, device_id=where,
+                            device_id_type=pl.DeviceIdType.MESH)
+
+    greet((seq, other))
+    greet((mate, rank))
+
+    @pl.when(has_before)
+    def _():
+        greet((seq - 2, rank))
+
+    @pl.when(has_after)
+    def _():
+        greet((seq + 2, rank))
+
+    @pl.when(jnp.logical_and(even, near_comes))
+    def _():
+        greet((near_from, rank))
+
+    @pl.when(jnp.logical_and(jnp.logical_not(even), near_goes))
+    def _():
+        greet((near_to, rank))
+
+    across = jnp.where(even, near_comes, near_goes)
+    pl.semaphore_wait(
+        barrier,
+        2 + has_before.astype(jnp.int32) + has_after.astype(jnp.int32) + across.astype(jnp.int32),
+    )
+
+    def arrive(g):
+        for a in range(4):
+            in_copy(a, g).start()
+            in_stay(a, g).start()
+
+    for g in range(AHEAD):
+        arrive(g)
+
+    def clear(buffer):
+        def one(g, _):
+            buffer[g] = jnp.zeros(buffer.shape[1:], buffer.dtype)
+            return 0
+
+        lax.fori_loop(0, heads, one, 0)
+
+    @pl.when(jnp.logical_not(has_before))
+    def _():
+        clear(mid)
+        clear(far)
+
+    @pl.when(jnp.logical_not(near_comes))
+    def _():
+        clear(near)
+
+    @pl.when(jnp.logical_not(near_goes))
+    def _():
+        clear(near_back)
+
+    @pl.when(jnp.logical_not(has_after))
+    def _():
+        clear(mid_back)
+
+    at_row = lax.broadcasted_iota(jnp.int32, (BLOCK, BLOCK), 0)
+    at_col = lax.broadcasted_iota(jnp.int32, (BLOCK, BLOCK), 1)
+    for w in range(4):
+        ok = docs_k[w] == docs_q[...]
+        if w == 3:
+            ok = jnp.logical_and(ok, at_row <= at_col)
+        bias[w] = jnp.where(ok, 0.0, NEGATIVE)
+
+    def spread(g):
+        for a in range(2):
+            in_arrival(a, g).wait_recv()
+            in_stay(a, g).wait()
+
+        @pl.when(has_after)
+        def _():
+            mid_copy(g).start()
+
+        @pl.when(near_goes)
+        def _():
+            near_copy(g).start()
+
+    def forward(g):
+        @pl.when(has_before)
+        def _():
+            mid_copy(g).wait_recv()
+            far_copy(g).start()
+
+    def compute(g):
+        for a in range(2, 4):
+            in_arrival(a, g).wait_recv()
+            in_stay(a, g).wait()
+
+        @pl.when(near_comes)
+        def _():
+            near_copy(g).wait_recv()
+
+        @pl.when(has_before)
+        def _():
+            far_copy(g).wait_recv()
+            far_copy(g).wait_send()
+
+        @pl.when(has_after)
+        def _():
+            mid_copy(g).wait_send()
+
+        @pl.when(near_goes)
+        def _():
+            near_copy(g).wait_send()
+
+        a, b = slots[0, g], slots[1, g]
+
+        def pick(n, which):
+            return jnp.where(
+                n == 0, near[g, which], jnp.where(n == 1, mid[g, which], far[g, which])
+            )
+
+        keys = [pick(a, 0), pick(b, 0), own[g, 0]]
+        values = [pick(a, 1), pick(b, 1), own[g, 1]]
+        biases = [bias[a], bias[b], bias[3]]
+        o, dq, dks, dvs = one_head(own[g, 2], own[g, 3], keys, values, biases)
+        own[g, 2] = o
+        own[g, 3] = dq
+        for which, d in ((0, dks), (1, dvs)):
+            own[g, which] = d[2].astype(jnp.bfloat16)
+            for w, buffer in enumerate((near, mid, far)):
+                here = jnp.where(a == w, d[0], jnp.where(b == w, d[1], 0.0))
+                buffer[g, which] = here.astype(jnp.bfloat16)
+
+        @pl.when(has_before)
+        def _():
+            mate_back_copy(g).start()
+
+        @pl.when(near_comes)
+        def _():
+            near_back_copy(g).start()
+
+        for a in range(2, 4):
+            out_copy(a, g).start()
+            out_stay(a, g).start()
+
+    def join(g):
+        @pl.when(has_before)
+        def _():
+            mate_back_copy(g).wait_recv()
+            both = mid[g].astype(jnp.float32) + mate_back[g].astype(jnp.float32)
+            mid[g] = both.astype(jnp.bfloat16)
+            mid_back_copy(g).start()
+
+    def finish(g):
+        @pl.when(near_goes)
+        def _():
+            near_back_copy(g).wait_recv()
+
+        @pl.when(has_after)
+        def _():
+            mid_back_copy(g).wait_recv()
+
+        total = (
+            own[g, pl.ds(0, 2)].astype(jnp.float32)
+            + near_back[g].astype(jnp.float32)
+            + mid_back[g].astype(jnp.float32)
+        )
+        own[g, pl.ds(0, 2)] = total.astype(jnp.bfloat16)
+        for a in range(2):
+            out_copy(a, g).start()
+            out_stay(a, g).start()
+
+    stages = ((arrive, -AHEAD), (spread, 0), (forward, LAGS[0]), (join, LAGS[2]),
+              (finish, LAGS[3]), (compute, LAGS[1]))
+
+    def step(t, _):
+        for stage, lag in stages:
+            g = t - lag
+
+            @pl.when(jnp.logical_and(g >= 0, g < heads))
+            def _():
+                stage(g)
+
+        return 0
+
+    lax.fori_loop(0, heads + LAGS[3], step, 0)
+
+    def drain(view, semaphore):
+        pltpu.make_async_copy(view, view, semaphore).wait()
+
+    for a in range(4):
+        drain(sources[a].at[:, group(other)], in_send.at[a])
+        drain(results[a].at[:, group(rank)], out_send.at[a])
+        drain(results[a].at[:, group(rank)], out_local.at[a])
+        drain(results[a].at[:, group(other)], out_recv.at[a])
+
+    @pl.when(has_before)
+    def _():
+        drain(far, back_send.at[0])
+        drain(mid, back_send.at[2])
+
+    @pl.when(near_comes)
+    def _():
+        drain(near, back_send.at[1])
+
+
+def whole_call(peers, length, slots, docs_q, docs_k, queries, key_rows, value_rows, out_grad):
+    heads = queries.shape[1] // peers // HEAD_DIM
+    window = pltpu.VMEM((heads, 2, BLOCK, HEAD_DIM), jnp.bfloat16)
+    dma = pltpu.SemaphoreType.DMA
+    hbm = pl.BlockSpec(memory_space=pl.ANY)
+    vmem = pl.BlockSpec(memory_space=pltpu.VMEM)
+    result = jax.ShapeDtypeStruct(queries.shape, jnp.bfloat16)
+    return pl.pallas_call(
+        functools.partial(whole_pass, peers, length),
+        in_specs=[pl.BlockSpec(memory_space=pltpu.SMEM), vmem, vmem, hbm, hbm, hbm, hbm],
+        out_specs=[hbm] * 4,
+        out_shape=[result] * 4,
+        scratch_shapes=[pltpu.VMEM((heads, 4, BLOCK, HEAD_DIM), jnp.bfloat16)]
+        + [window] * 6
+        + [pltpu.VMEM((4, BLOCK, BLOCK), jnp.float32)]
+        + [dma((4,)), dma((4, heads)), dma((4, heads))]
+        + [dma((heads,))] * 6
+        + [dma((3,))]
+        + [dma((heads,))] * 3
+        + [dma((4,))] * 3,
+        compiler_params=pltpu.CompilerParams(
+            collective_id=0, has_side_effects=True, vmem_limit_bytes=60 * 2**20
+        ),
+        cost_estimate=pl.CostEstimate(
+            flops=heads * 12 * 128 * 512 * 1536,
+            bytes_accessed=16 * 2**20,
+            transcendentals=heads * 512 * 1536,
+        ),
+    )(slots, docs_q, docs_k, queries, key_rows, value_rows, out_grad)
+
+
 def per_device(queries, key_rows, value_rows, out_grad, doc_ids, picks):
     peers = lax.axis_size("head")
     length = lax.axis_size("seq")
@@ -186,6 +505,11 @@
     )
     docs_q = docs_k[3:4]
     docs_k = docs_k[:, :, None]
+
+    if peers == 2 and length % 2 == 0:
+        return whole_call(
+            peers, length, slots, docs_q, docs_k, queries, key_rows, value_rows, out_grad
+        )
 
     per = heads // chunks
     outs, grads = [], []

time: 407 us -> 243 us (0.60)
  waiting for transfers between devices: 217 us -> 0 us
  Pallas kernels: 60.4 us -> 219 us
  other arithmetic: 42.1 us -> 1.34 us
  local copies, waits for them, and re-layouts: 46.2 us -> 12.3 us
  starting transfers between devices: 32.3 us -> 0 us
    ppermute x20 -> x0, waiting for transfers between devices: 217 us -> none  [the longest x2 97 us: per_device(): from_mid = lax.ppermute(joined, 'seq', back(two))]
    pallas_call x2 -> x1, Pallas kernels: 60.4 us -> 219 us  [whole_call(): pl.pallas_call(functools.partial(whole_pass, peers, length), in_specs=[pl...]
    ppermute x20 -> x0, starting transfers between devices: 32.3 us -> none  [the longest x2 6.83 us: per_device(): mid = lax.ppermute(own, 'seq', two)]
    another operation x12 -> x0, local copies, waits for them, and re-layouts: 17.4 us -> none  [the longest x8 15.1 us: whole(): x = jnp.stack([p[which] for p in pieces], axis=2)]
    convert_element_type x4 -> x0, other arithmetic: 16.4 us -> none  [the longest x2 8.64 us: per_device(): total = (parts[3].astype(jnp.float32) + from_near.astype(jnp.float32) + f...]
    select_n x7 -> x0, other arithmetic: 16.4 us -> none  [the longest x4 14 us: gather_heads(): jnp.where(rank == 0, jnp.concatenate([mine, theirs], axis=1), jnp.concate...]
    unnamed x22 -> x12, local copies, waits for them, and re-layouts: 18.8 us -> 9.3 us
    another operation x6 -> x0, other arithmetic: 9.18 us -> none  [the longest x2 5.64 us: gather_heads(): x = jnp.stack(arrays)]
  transfers between devices with their start and end apart: 20 -> 0, of which waited for: 10 -> 0; matrix products, arithmetic and copies ran while one was open for 11% -> 0% of each run, Pallas kernels for 15% -> 0%
where the time goes in v2:
time: 243 us; the launch traced here: 241 us
  Pallas kernels  219 us (90%)
  local copies, waits for them, and re-layouts  12.3 us (5%)
  between operations  8.57 us (4%)
    pallas_call x1, Pallas kernels, whole_call(): pl.pallas_call(functools.partial(whole_pass, peers, length), in_specs=[pl...  219 us
    unnamed x12, local copies, waits for them, and re-layouts  9.3 us

profile of v2, /device:TPU:20, one launch (start us, length us, event | category | flops | bytes accessed | tf_op | source)
XLA Modules:
  0.0 240.8 jit_solution(9972456391759262777)
XLA Ops:
  0.7 0.1 fusion.1
  0.7 1.2 fusion.slots
  2.0 0.7 fusion.2
  10.5 1.0 pad_dynamic-slice_fusion.2
  11.5 0.0 copy-start.3
  11.5 1.3 copy.10.docs_k
  12.9 0.0 copy-done.3
  12.9 218.7 %shard_map.93 = (bf16[256,4096]{1,0:T(8,128)(2,1)}, bf16[256,4096]{1,0:T(8,128)(2,1)}, bf16[256,4096]{1,0:T(8,128)(2,1)}, bf16[256,4096]{1,0:T(8,128)(2,1)}) custom-call(s32[2,16]{1,0:T(2,128)} %fusion.slots, s32[1,512]{1,0:T(1,128)} %bitcast.17, s32[4,512,1]{2,1,0:T(8,128)} %copy.10.docs_k, bf16[256,4096]{1,0:T(8,128)(2,1)} %q_ref.1, ...), custom_call_target="tpu_custom_call" | custom-call | flops 19327352832 | bytes 16777216 | tf_op jit(solution)/shard_map/pallas_call | solution.py:415
  231.5 0.0 copy-start.2
  231.5 3.3 %copy.15 = bf16[256,4096]{1,0:T(8,128)(2,1)} copy(bf16[256,4096]{1,0:T(8,128)(2,1)} %get-tuple-element.16) | data formatting | bytes 4194304
  234.8 0.0 copy-done.2
  234.8 0.0 copy-start.1
  234.8 1.3 copy.16
  236.1 1.0 copy-done.1
  237.2 0.0 copy-start
  237.2 1.3 copy.17
  238.5 1.0 copy-done
  239.5 1.3 copy.18
  (1 shorter events, 0.0 us)
Async XLA Ops:
  11.5 1.4 copy-start.3
  231.5 3.3 %copy-start.2 = (bf16[256,4096]{1,0:T(8,128)(2,1)S(1)}, bf16[256,4096]{1,0:T(8,128)(2,1)}, u32[]{:S(2)}) copy-start(bf16[256,4096]{1,0:T(8,128)(2,1)} %get-tuple-element.17) | copy-start | bytes 6291460
  234.8 2.3 copy-start.1
  237.2 2.3 copy-start

commit v3 on v2

--- a/solution.py
+++ b/solution.py
@@ -11,8 +11,8 @@
 REACH = 3
 NEGATIVE = -1e30
 CHUNKS = 2
-AHEAD = 2
-LAGS = (2, 3, 4, 6)
+AHEAD = 4
+LAGS = (2, 4, 5, 7)
 
 
 def nt(a, b):
@@ -119,7 +119,7 @@
     )(slots, docs_q, docs_k, qg, own, near, mid, far)
 
 
-def whole_pass(peers, length, slots, docs_q, docs_k, q_ref, k_ref, v_ref, g_ref,
+def whole_pass(peers, length, picks, docs, q_ref, k_ref, v_ref, g_ref,
                o_out, dq_out, dk_out, dv_out,
                own, near, mid, far, mate_back, near_back, mid_back, bias,
                in_send, in_recv, in_local, near_send, near_recv, mid_send, mid_recv,
@@ -233,12 +233,18 @@
     )
 
     def arrive(g):
-        for a in range(4):
+        for a in range(2):
             in_copy(a, g).start()
             in_stay(a, g).start()
 
+    def follow(g):
+        for a in range(2, 4):
+            in_copy(a, g).start()
+            in_stay(a, g).start()
+
     for g in range(AHEAD):
         arrive(g)
+    follow(0)
 
     def clear(buffer):
         def one(g, _):
@@ -264,13 +270,20 @@
     def _():
         clear(mid_back)
 
+    offsets = (jnp.where(even, 3, 1), 2, jnp.where(even, 1, 3), 0)
     at_row = lax.broadcasted_iota(jnp.int32, (BLOCK, BLOCK), 0)
     at_col = lax.broadcasted_iota(jnp.int32, (BLOCK, BLOCK), 1)
     for w in range(4):
-        ok = docs_k[w] == docs_q[...]
+        block = seq - offsets[w]
+        ids = jnp.where(block >= 0, docs[jnp.maximum(block, 0)], -1)
+        tall = jnp.broadcast_to(ids.astype(jnp.float32), (HEAD_DIM, BLOCK)).T[:, :1]
+        ok = tall == docs[seq].astype(jnp.float32)
         if w == 3:
             ok = jnp.logical_and(ok, at_row <= at_col)
         bias[w] = jnp.where(ok, 0.0, NEGATIVE)
+
+    def slot(pick):
+        return jnp.where(pick == 2, 1, jnp.where(pick == offsets[0], 0, 2))
 
     def spread(g):
         for a in range(2):
@@ -313,7 +326,7 @@
         def _():
             near_copy(g).wait_send()
 
-        a, b = slots[0, g], slots[1, g]
+        a, b = slot(picks[0, g, 0]), slot(picks[0, g, 1])
 
         def pick(n, which):
             return jnp.where(
@@ -371,8 +384,8 @@
             out_copy(a, g).start()
             out_stay(a, g).start()
 
-    stages = ((arrive, -AHEAD), (spread, 0), (forward, LAGS[0]), (join, LAGS[2]),
-              (finish, LAGS[3]), (compute, LAGS[1]))
+    stages = ((arrive, -AHEAD), (follow, -1), (spread, 0), (forward, LAGS[0]),
+              (compute, LAGS[1]), (join, LAGS[2]), (finish, LAGS[3]))
 
     def step(t, _):
         for stage, lag in stages:
@@ -405,7 +418,7 @@
         drain(near, back_send.at[1])
 
 
-def whole_call(peers, length, slots, docs_q, docs_k, queries, key_rows, value_rows, out_grad):
+def whole_call(peers, length, picks, docs, queries, key_rows, value_rows, out_grad):
     heads = queries.shape[1] // peers // HEAD_DIM
     window = pltpu.VMEM((heads, 2, BLOCK, HEAD_DIM), jnp.bfloat16)
     dma = pltpu.SemaphoreType.DMA
@@ -414,7 +427,7 @@
     result = jax.ShapeDtypeStruct(queries.shape, jnp.bfloat16)
     return pl.pallas_call(
         functools.partial(whole_pass, peers, length),
-        in_specs=[pl.BlockSpec(memory_space=pltpu.SMEM), vmem, vmem, hbm, hbm, hbm, hbm],
+        in_specs=[pl.BlockSpec(memory_space=pltpu.SMEM), vmem, hbm, hbm, hbm, hbm],
         out_specs=[hbm] * 4,
         out_shape=[result] * 4,
         scratch_shapes=[pltpu.VMEM((heads, 4, BLOCK, HEAD_DIM), jnp.bfloat16)]
@@ -433,7 +446,7 @@
             bytes_accessed=16 * 2**20,
             transcendentals=heads * 512 * 1536,
         ),
-    )(slots, docs_q, docs_k, queries, key_rows, value_rows, out_grad)
+    )(picks, docs, queries, key_rows, value_rows, out_grad)
 
 
 def per_device(queries, key_rows, value_rows, out_grad, doc_ids, picks):
@@ -508,7 +521,8 @@
 
     if peers == 2 and length % 2 == 0:
         return whole_call(
-            peers, length, slots, docs_q, docs_k, queries, key_rows, value_rows, out_grad
+            peers, length, picks, doc_ids.reshape(-1, 1, BLOCK), queries, key_rows, value_rows,
+            out_grad,
         )
 
     per = heads // chunks

time: 243 us -> 224 us (0.922)
  between operations: 8.57 us -> 0.65 us
  Pallas kernels: 219 us -> 212 us
    pallas_call x1, Pallas kernels: 219 us -> 212 us  [whole_call(): pl.pallas_call(functools.partial(whole_pass, peers, length), in_specs=[pl...]
    unnamed x12 -> x11, local copies, waits for them, and re-layouts: 9.3 us -> 10.6 us
where the time goes in v3:
time: 224 us
  Pallas kernels  212 us (95%)
  local copies, waits for them, and re-layouts  10.6 us (5%)
    pallas_call x1, Pallas kernels, whole_call(): pl.pallas_call(functools.partial(whole_pass, peers, length), in_specs=[pl...  212 us
    unnamed x11, local copies, waits for them, and re-layouts  10.6 us

profile of v3, /device:TPU:20, one launch (start us, length us, event | category | flops | bytes accessed | tf_op | source)
XLA Modules:
  0.0 223.7 jit_solution(6431613837497996407)
XLA Ops:
  0.6 1.4 copy.10.picks
  2.0 212.4 %shard_map.93 = (bf16[256,4096]{1,0:T(8,128)(2,1)}, bf16[256,4096]{1,0:T(8,128)(2,1)}, bf16[256,4096]{1,0:T(8,128)(2,1)}, bf16[256,4096]{1,0:T(8,128)(2,1)}) custom-call(s32[1,16,2]{2,1,0:T(8,128)} %copy.10.picks, s32[16,1,512]{2,1,0:T(1,128)} %bitcast.1, bf16[256,4096]{1,0:T(8,128)(2,1)} %q_ref.1, bf16[256,4096]{1,0:T(8,128)(2,1)} %k_ref.1, ...), custom_call_target="tpu_custom_call" | custom-call | flops 19327352832 | bytes 16777216 | tf_op jit(solution)/shard_map/pallas_call | solution.py:428
  214.4 0.0 copy-start.2
  214.4 3.3 %copy.15 = bf16[256,4096]{1,0:T(8,128)(2,1)} copy(bf16[256,4096]{1,0:T(8,128)(2,1)} %get-tuple-element.8) | data formatting | bytes 4194304
  217.7 0.0 copy-done.2
  217.7 0.0 copy-start.1
  217.7 1.3 copy.16
  219.0 1.0 copy-done.1
  220.1 0.0 copy-start
  220.1 1.3 copy.17
  221.4 1.0 copy-done
  222.4 1.3 copy.18
Async XLA Ops:
  214.4 3.3 %copy-start.2 = (bf16[256,4096]{1,0:T(8,128)(2,1)S(1)}, bf16[256,4096]{1,0:T(8,128)(2,1)}, u32[]{:S(2)}) copy-start(bf16[256,4096]{1,0:T(8,128)(2,1)} %get-tuple-element.9) | copy-start | bytes 6291460
  217.7 2.3 %copy-start.1 = (bf16[256,4096]{1,0:T(8,128)(2,1)S(1)}, bf16[256,4096]{1,0:T(8,128)(2,1)}, u32[]{:S(2)}) copy-start(bf16[256,4096]{1,0:T(8,128)(2,1)} %get-tuple-element.10) | copy-start | bytes 6291460
  220.1 2.3 %copy-start = (bf16[256,4096]{1,0:T(8,128)(2,1)S(1)}, bf16[256,4096]{1,0:T(8,128)(2,1)}, u32[]{:S(2)}) copy-start(bf16[256,4096]{1,0:T(8,128)(2,1)} %get-tuple-element.11) | copy-start | bytes 6291460

commit v4 on v3

--- a/solution.py
+++ b/solution.py
@@ -11,8 +11,9 @@
 REACH = 3
 NEGATIVE = -1e30
 CHUNKS = 2
+PAIR = 2 * HEAD_DIM
 AHEAD = 4
-LAGS = (2, 4, 5, 7)
+LAGS = (2, 3, 4, 6)
 
 
 def nt(a, b):
@@ -128,7 +129,7 @@
     seq = lax.axis_index("seq")
     rank = lax.axis_index("head")
     other = 1 - rank
-    heads = own.shape[0]
+    heads = near.shape[0]
     rows = q_ref.shape[0]
     width = heads * HEAD_DIM
     parity = lax.rem(seq, 2)
@@ -152,8 +153,25 @@
     def token_rows(r):
         return pl.ds(pl.multiple_of(r * rows, rows), rows)
 
-    def columns(r, g):
-        return pl.ds(pl.multiple_of(r * width + g * HEAD_DIM, HEAD_DIM), HEAD_DIM)
+    def columns(r, p):
+        return pl.ds(pl.multiple_of(r * width + p * PAIR, PAIR), PAIR)
+
+    def place(g):
+        return lax.div(g, 2), pl.ds(pl.multiple_of(lax.rem(g, 2) * HEAD_DIM, HEAD_DIM), HEAD_DIM)
+
+    def own_keys(g):
+        p, lanes = place(g)
+        return own.at[p, pl.ds(0, 2), :, lanes]
+
+    def on_first(g, act):
+        @pl.when(lax.rem(g, 2) == 0)
+        def _():
+            act(lax.div(g, 2))
+
+    def on_second(g, act):
+        @pl.when(lax.rem(g, 2) == 1)
+        def _():
+            act(lax.div(g, 2))
 
     def group(r):
         return pl.ds(pl.multiple_of(r * width, width), width)
@@ -171,11 +189,11 @@
                                      own.at[g, a, token_rows(rank), :], in_local.at[a, g])
 
     def near_copy(g):
-        return copy(own.at[g, pl.ds(0, 2)], near.at[g], near_send.at[g], near_recv.at[g],
+        return copy(own_keys(g), near.at[g], near_send.at[g], near_recv.at[g],
                     (near_to, rank))
 
     def mid_copy(g):
-        return copy(own.at[g, pl.ds(0, 2)], mid.at[g], mid_send.at[g], mid_recv.at[g],
+        return copy(own_keys(g), mid.at[g], mid_send.at[g], mid_recv.at[g],
                     (seq + 2, rank))
 
     def far_copy(g):
@@ -232,19 +250,39 @@
         2 + has_before.astype(jnp.int32) + has_after.astype(jnp.int32) + across.astype(jnp.int32),
     )
 
+    def enter(low):
+        def act(p):
+            for a in range(low, low + 2):
+                in_copy(a, p).start()
+                in_stay(a, p).start()
+
+        return act
+
+    def entered(low):
+        def act(p):
+            for a in range(low, low + 2):
+                in_arrival(a, p).wait_recv()
+                in_stay(a, p).wait()
+
+        return act
+
+    def leave(low):
+        def act(p):
+            for a in range(low, low + 2):
+                out_copy(a, p).start()
+                out_stay(a, p).start()
+
+        return act
+
     def arrive(g):
-        for a in range(2):
-            in_copy(a, g).start()
-            in_stay(a, g).start()
+        on_first(g, enter(0))
 
     def follow(g):
-        for a in range(2, 4):
-            in_copy(a, g).start()
-            in_stay(a, g).start()
-
-    for g in range(AHEAD):
-        arrive(g)
-    follow(0)
+        on_first(g, enter(2))
+
+    for p in range(AHEAD // 2):
+        enter(0)(p)
+    enter(2)(0)
 
     def clear(buffer):
         def one(g, _):
@@ -286,9 +324,7 @@
         return jnp.where(pick == 2, 1, jnp.where(pick == offsets[0], 0, 2))
 
     def spread(g):
-        for a in range(2):
-            in_arrival(a, g).wait_recv()
-            in_stay(a, g).wait()
+        on_first(g, entered(0))
 
         @pl.when(has_after)
         def _():
@@ -305,9 +341,7 @@
             far_copy(g).start()
 
     def compute(g):
-        for a in range(2, 4):
-            in_arrival(a, g).wait_recv()
-            in_stay(a, g).wait()
+        on_first(g, entered(2))
 
         @pl.when(near_comes)
         def _():
@@ -333,14 +367,17 @@
                 n == 0, near[g, which], jnp.where(n == 1, mid[g, which], far[g, which])
             )
 
-        keys = [pick(a, 0), pick(b, 0), own[g, 0]]
-        values = [pick(a, 1), pick(b, 1), own[g, 1]]
+        p, lanes = place(g)
+        keys = [pick(a, 0), pick(b, 0), own[p, 0, :, lanes]]
+        values = [pick(a, 1), pick(b, 1), own[p, 1, :, lanes]]
         biases = [bias[a], bias[b], bias[3]]
-        o, dq, dks, dvs = one_head(own[g, 2], own[g, 3], keys, values, biases)
-        own[g, 2] = o
-        own[g, 3] = dq
+        o, dq, dks, dvs = one_head(
+            own[p, 2, :, lanes], own[p, 3, :, lanes], keys, values, biases
+        )
+        own[p, 2, :, lanes] = o
+        own[p, 3, :, lanes] = dq
         for which, d in ((0, dks), (1, dvs)):
-            own[g, which] = d[2].astype(jnp.bfloat16)
+            own[p, which, :, lanes] = d[2].astype(jnp.bfloat16)
             for w, buffer in enumerate((near, mid, far)):
                 here = jnp.where(a == w, d[0], jnp.where(b == w, d[1], 0.0))
                 buffer[g, which] = here.astype(jnp.bfloat16)
@@ -353,9 +390,7 @@
         def _():
             near_back_copy(g).start()
 
-        for a in range(2, 4):
-            out_copy(a, g).start()
-            out_stay(a, g).start()
+        on_second(g, leave(2))
 
     def join(g):
         @pl.when(has_before)
@@ -374,17 +409,16 @@
         def _():
             mid_back_copy(g).wait_recv()
 
+        p, lanes = place(g)
         total = (
-            own[g, pl.ds(0, 2)].astype(jnp.float32)
+            own[p, pl.ds(0, 2), :, lanes].astype(jnp.float32)
             + near_back[g].astype(jnp.float32)
             + mid_back[g].astype(jnp.float32)
         )
-        own[g, pl.ds(0, 2)] = total.astype(jnp.bfloat16)
-        for a in range(2):
-            out_copy(a, g).start()
-            out_stay(a, g).start()
-
-    stages = ((arrive, -AHEAD), (follow, -1), (spread, 0), (forward, LAGS[0]),
+        own[p, pl.ds(0, 2), :, lanes] = total.astype(jnp.bfloat16)
+        on_second(g, leave(0))
+
+    stages = ((arrive, -AHEAD), (follow, -2), (spread, 0), (forward, LAGS[0]),
               (compute, LAGS[1]), (join, LAGS[2]), (finish, LAGS[3]))
 
     def step(t, _):
@@ -430,10 +464,10 @@
         in_specs=[pl.BlockSpec(memory_space=pltpu.SMEM), vmem, hbm, hbm, hbm, hbm],
         out_specs=[hbm] * 4,
         out_shape=[result] * 4,
-        scratch_shapes=[pltpu.VMEM((heads, 4, BLOCK, HEAD_DIM), jnp.bfloat16)]
+        scratch_shapes=[pltpu.VMEM((heads // 2, 4, BLOCK, PAIR), jnp.bfloat16)]
         + [window] * 6
         + [pltpu.VMEM((4, BLOCK, BLOCK), jnp.float32)]
-        + [dma((4,)), dma((4, heads)), dma((4, heads))]
+        + [dma((4,)), dma((4, heads // 2)), dma((4, heads // 2))]
         + [dma((heads,))] * 6
         + [dma((3,))]
         + [dma((heads,))] * 3
@@ -519,7 +553,7 @@
     docs_q = docs_k[3:4]
     docs_k = docs_k[:, :, None]
 
-    if peers == 2 and length % 2 == 0:
+    if peers == 2 and length % 2 == 0 and heads % 2 == 0:
         return whole_call(
             peers, length, picks, doc_ids.reshape(-1, 1, BLOCK), queries, key_rows, value_rows,
             out_grad,

time: 224 us -> 233 us (1.040)
  Pallas kernels: 212 us -> 220 us
    pallas_call x1, Pallas kernels: 212 us -> 220 us  [whole_call(): pl.pallas_call(functools.partial(whole_pass, peers, length), in_specs=[pl...]
where the time goes in v4:
time: 233 us; the launch traced here: 232 us
  Pallas kernels  220 us (94%)
  local copies, waits for them, and re-layouts  10.6 us (5%)
    pallas_call x1, Pallas kernels, whole_call(): pl.pallas_call(functools.partial(whole_pass, peers, length), in_specs=[pl...  220 us
    unnamed x11, local copies, waits for them, and re-layouts  10.6 us

profile of v4, /device:TPU:20, one launch (start us, length us, event | category | flops | bytes accessed | tf_op | source)
XLA Modules:
  0.0 231.7 jit_solution(16242477302292495023)
XLA Ops:
  0.6 1.4 copy.10.picks
  2.0 220.4 %shard_map.93 = (bf16[256,4096]{1,0:T(8,128)(2,1)}, bf16[256,4096]{1,0:T(8,128)(2,1)}, bf16[256,4096]{1,0:T(8,128)(2,1)}, bf16[256,4096]{1,0:T(8,128)(2,1)}) custom-call(s32[1,16,2]{2,1,0:T(8,128)} %copy.10.picks, s32[16,1,512]{2,1,0:T(1,128)} %bitcast.1, bf16[256,4096]{1,0:T(8,128)(2,1)} %q_ref.1, bf16[256,4096]{1,0:T(8,128)(2,1)} %k_ref.1, ...), custom_call_target="tpu_custom_call" | custom-call | flops 19327352832 | bytes 16777216 | tf_op jit(solution)/shard_map/pallas_call | solution.py:462
  222.4 0.0 copy-start.2
  222.4 3.3 %copy.15 = bf16[256,4096]{1,0:T(8,128)(2,1)} copy(bf16[256,4096]{1,0:T(8,128)(2,1)} %get-tuple-element.8) | data formatting | bytes 4194304
  225.7 0.0 copy-done.2
  225.7 0.0 copy-start.1
  225.7 1.3 copy.16
  227.0 1.0 copy-done.1
  228.0 0.0 copy-start
  228.0 1.3 copy.17
  229.3 1.0 copy-done
  230.4 1.3 copy.18
Async XLA Ops:
  222.4 3.3 %copy-start.2 = (bf16[256,4096]{1,0:T(8,128)(2,1)S(1)}, bf16[256,4096]{1,0:T(8,128)(2,1)}, u32[]{:S(2)}) copy-start(bf16[256,4096]{1,0:T(8,128)(2,1)} %get-tuple-element.9) | copy-start | bytes 6291460
  225.7 2.3 %copy-start.1 = (bf16[256,4096]{1,0:T(8,128)(2,1)S(1)}, bf16[256,4096]{1,0:T(8,128)(2,1)}, u32[]{:S(2)}) copy-start(bf16[256,4096]{1,0:T(8,128)(2,1)} %get-tuple-element.10) | copy-start | bytes 6291460
  228.0 2.3 %copy-start = (bf16[256,4096]{1,0:T(8,128)(2,1)S(1)}, bf16[256,4096]{1,0:T(8,128)(2,1)}, u32[]{:S(2)}) copy-start(bf16[256,4096]{1,0:T(8,128)(2,1)} %get-tuple-element.11) | copy-start | bytes 6291460

commit v5 on v3

--- a/solution.py
+++ b/solution.py
@@ -11,8 +11,8 @@
 REACH = 3
 NEGATIVE = -1e30
 CHUNKS = 2
-AHEAD = 4
-LAGS = (2, 4, 5, 7)
+AHEAD = 6
+LAGS = (3, 6, 7, 9)
 
 
 def nt(a, b):

time: 224 us -> 227 us (1.013)
  no operation moved by 1% of the time
where the time goes in v5:
time: 227 us; the launch traced here: 225 us
  Pallas kernels  214 us (94%)
  local copies, waits for them, and re-layouts  10.6 us (5%)
    pallas_call x1, Pallas kernels, whole_call(): pl.pallas_call(functools.partial(whole_pass, peers, length), in_specs=[pl...  214 us
    unnamed x11, local copies, waits for them, and re-layouts  10.6 us

profile of v5, /device:TPU:20, one launch (start us, length us, event | category | flops | bytes accessed | tf_op | source)
XLA Modules:
  0.0 225.3 jit_solution(4353740059930196011)
XLA Ops:
  0.6 1.4 copy.10.picks
  2.0 214.0 %shard_map.93 = (bf16[256,4096]{1,0:T(8,128)(2,1)}, bf16[256,4096]{1,0:T(8,128)(2,1)}, bf16[256,4096]{1,0:T(8,128)(2,1)}, bf16[256,4096]{1,0:T(8,128)(2,1)}) custom-call(s32[1,16,2]{2,1,0:T(8,128)} %copy.10.picks, s32[16,1,512]{2,1,0:T(1,128)} %bitcast.1, bf16[256,4096]{1,0:T(8,128)(2,1)} %q_ref.1, bf16[256,4096]{1,0:T(8,128)(2,1)} %k_ref.1, ...), custom_call_target="tpu_custom_call" | custom-call | flops 19327352832 | bytes 16777216 | tf_op jit(solution)/shard_map/pallas_call | solution.py:428
  216.0 0.0 copy-start.2
  216.0 3.3 %copy.15 = bf16[256,4096]{1,0:T(8,128)(2,1)} copy(bf16[256,4096]{1,0:T(8,128)(2,1)} %get-tuple-element.8) | data formatting | bytes 4194304
  219.3 0.0 copy-done.2
  219.3 0.0 copy-start.1
  219.3 1.3 copy.16
  220.6 1.0 copy-done.1
  221.7 0.0 copy-start
  221.7 1.3 copy.17
  223.0 1.0 copy-done
  224.0 1.3 copy.18
Async XLA Ops:
  216.0 3.3 %copy-start.2 = (bf16[256,4096]{1,0:T(8,128)(2,1)S(1)}, bf16[256,4096]{1,0:T(8,128)(2,1)}, u32[]{:S(2)}) copy-start(bf16[256,4096]{1,0:T(8,128)(2,1)} %get-tuple-element.9) | copy-start | bytes 6291460
  219.3 2.3 %copy-start.1 = (bf16[256,4096]{1,0:T(8,128)(2,1)S(1)}, bf16[256,4096]{1,0:T(8,128)(2,1)}, u32[]{:S(2)}) copy-start(bf16[256,4096]{1,0:T(8,128)(2,1)} %get-tuple-element.10) | copy-start | bytes 6291460
  221.7 2.3 %copy-start = (bf16[256,4096]{1,0:T(8,128)(2,1)S(1)}, bf16[256,4096]{1,0:T(8,128)(2,1)}, u32[]{:S(2)}) copy-start(bf16[256,4096]{1,0:T(8,128)(2,1)} %get-tuple-element.11) | copy-start | bytes 6291460

commit v6 on v3

--- a/solution.py
+++ b/solution.py
@@ -12,7 +12,7 @@
 NEGATIVE = -1e30
 CHUNKS = 2
 AHEAD = 4
-LAGS = (2, 4, 5, 7)
+LAGS = (2, 4, 5, 8)
 
 
 def nt(a, b):
@@ -349,10 +349,6 @@
         def _():
             mate_back_copy(g).start()
 
-        @pl.when(near_comes)
-        def _():
-            near_back_copy(g).start()
-
         for a in range(2, 4):
             out_copy(a, g).start()
             out_stay(a, g).start()
@@ -364,6 +360,10 @@
             both = mid[g].astype(jnp.float32) + mate_back[g].astype(jnp.float32)
             mid[g] = both.astype(jnp.bfloat16)
             mid_back_copy(g).start()
+
+        @pl.when(near_comes)
+        def _():
+            near_back_copy(g).start()
 
     def finish(g):
         @pl.when(near_goes)

time: 224 us -> 237 us (1.058); the launches traced: 224 us -> 234 us
  Pallas kernels: 212 us -> 223 us
    pallas_call x1, Pallas kernels: 212 us -> 223 us  [whole_call(): pl.pallas_call(functools.partial(whole_pass, peers, length), in_specs=[pl...]
where the time goes in v6:
time: 237 us; the launch traced here: 234 us
  Pallas kernels  223 us (94%)
  local copies, waits for them, and re-layouts  10.6 us (4%)
    pallas_call x1, Pallas kernels, whole_call(): pl.pallas_call(functools.partial(whole_pass, peers, length), in_specs=[pl...  223 us
    unnamed x11, local copies, waits for them, and re-layouts  10.6 us

profile of v6, /device:TPU:20, one launch (start us, length us, event | category | flops | bytes accessed | tf_op | source)
XLA Modules:
  0.0 234.0 jit_solution(2351244377301677876)
XLA Ops:
  0.6 1.4 copy.10.picks
  2.0 222.7 %shard_map.93 = (bf16[256,4096]{1,0:T(8,128)(2,1)}, bf16[256,4096]{1,0:T(8,128)(2,1)}, bf16[256,4096]{1,0:T(8,128)(2,1)}, bf16[256,4096]{1,0:T(8,128)(2,1)}) custom-call(s32[1,16,2]{2,1,0:T(8,128)} %copy.10.picks, s32[16,1,512]{2,1,0:T(1,128)} %bitcast.1, bf16[256,4096]{1,0:T(8,128)(2,1)} %q_ref.1, bf16[256,4096]{1,0:T(8,128)(2,1)} %k_ref.1, ...), custom_call_target="tpu_custom_call" | custom-call | flops 19327352832 | bytes 16777216 | tf_op jit(solution)/shard_map/pallas_call | solution.py:428
  224.7 0.0 copy-start.2
  224.7 3.3 %copy.15 = bf16[256,4096]{1,0:T(8,128)(2,1)} copy(bf16[256,4096]{1,0:T(8,128)(2,1)} %get-tuple-element.8) | data formatting | bytes 4194304
  227.9 0.0 copy-done.2
  227.9 0.0 copy-start.1
  227.9 1.3 copy.16
  229.3 1.0 copy-done.1
  230.3 0.0 copy-start
  230.3 1.3 copy.17
  231.6 1.0 copy-done
  232.6 1.3 copy.18
Async XLA Ops:
  224.7 3.3 %copy-start.2 = (bf16[256,4096]{1,0:T(8,128)(2,1)S(1)}, bf16[256,4096]{1,0:T(8,128)(2,1)}, u32[]{:S(2)}) copy-start(bf16[256,4096]{1,0:T(8,128)(2,1)} %get-tuple-element.9) | copy-start | bytes 6291460
  227.9 2.3 %copy-start.1 = (bf16[256,4096]{1,0:T(8,128)(2,1)S(1)}, bf16[256,4096]{1,0:T(8,128)(2,1)}, u32[]{:S(2)}) copy-start(bf16[256,4096]{1,0:T(8,128)(2,1)} %get-tuple-element.10) | copy-start | bytes 6291460
  230.3 2.3 %copy-start = (bf16[256,4096]{1,0:T(8,128)(2,1)S(1)}, bf16[256,4096]{1,0:T(8,128)(2,1)}, u32[]{:S(2)}) copy-start(bf16[256,4096]{1,0:T(8,128)(2,1)} %get-tuple-element.11) | copy-start | bytes 6291460
